TPU v7x, 256 devices: a whole 4x4x8 slice. The times are simulated.
256 devices in a mesh: row: 16 (over z, y_lo), col: 16 (over x, y_hi, core).
Axes of the slice: x: 4, y: 4 (y_hi: 2, y_lo: 2; y = y_hi * 2 + y_lo), z: 8, core: 2. Of those that a mesh axis runs over, the one named last changes fastest.
Arguments:
- left_proj: bfloat16 [512, 512, 128], P('row', 'col'), may hold values from -6 to 6
- right_proj: bfloat16 [512, 512, 128], P('col', 'row'), may hold values from -6 to 6
- gate: bfloat16 [512, 512, 128], P('row', 'col'), may hold values from -8 to 8
- out_weight: bfloat16 [128, 128], replicated, may hold values from -0.5 to 0.5
- grad_out: bfloat16 [512, 512, 128], P('row', 'col'), may hold values from -6 to 6
Outputs:
- grad_left: bfloat16 [512, 512, 128], P('row', 'col')
- grad_right: bfloat16 [512, 512, 128], P('col', 'row')
- grad_gate: bfloat16 [512, 512, 128], P('row', 'col')
- grad_weight: float32 [128, 128], replicated
All inputs are finite; a program needn't handle non-finite values.
Results may differ from a plain program's by a relative error of at most 0.0057.
Values may be sent and summed in bfloat16 or wider, within the bound.
No kernel may reach another device: no remote copies, remote signals or barrier semaphores. Data moves between devices by JAX's collectives and lax.ppermute only.
A program may use at most 128 MiB of HBM per device.

v0:
```python
import jax
import jax.numpy as jnp
from jax import lax
from jax.sharding import PartitionSpec as P


def local(left_proj, right_proj, gate, out_weight, grad_out):
    left_full = lax.all_gather(left_proj, "col", axis=1, tiled=True)
    right_full = lax.all_gather(right_proj, "row", axis=1, tiled=True)
    tokens_all = left_full.shape[1]
    pair = jnp.einsum("ikc,jkc->ijc", left_full, right_full, preferred_element_type=jnp.float32)
    average = jnp.mean(pair, axis=-1, keepdims=True)
    centered = pair - average
    variance = jnp.mean(centered * centered, axis=-1, keepdims=True)
    inv_std = lax.rsqrt(variance + 1e-05)
    normed = centered * inv_std
    normed_half = normed.astype(jnp.bfloat16)
    gate_prob = jax.nn.sigmoid(gate.astype(jnp.float32))
    upstream = grad_out.astype(jnp.float32)
    gated_grad = (upstream * gate_prob).astype(jnp.bfloat16)
    projected = jnp.einsum(
        "ijc,cd->ijd", normed_half, out_weight, preferred_element_type=jnp.float32
    )
    grad_gate = (upstream * projected * gate_prob * (1.0 - gate_prob)).astype(jnp.bfloat16)
    weight_terms = (
        jnp.einsum("ijc,ijd->cd", normed_half, gated_grad, preferred_element_type=jnp.float32)
        / tokens_all
    )
    grad_weight = lax.psum(weight_terms, ("row", "col"))
    grad_normed = jnp.einsum(
        "ijd,cd->ijc", gated_grad, out_weight, preferred_element_type=jnp.float32
    )
    mean_one = jnp.mean(grad_normed, axis=-1, keepdims=True)
    mean_two = jnp.mean(grad_normed * normed, axis=-1, keepdims=True)
    grad_pair = ((grad_normed - mean_one - normed * mean_two) * inv_std).astype(jnp.bfloat16)
    left_sum = lax.psum_scatter(
        jnp.einsum("ijc,jkc->kic", grad_pair, right_full, preferred_element_type=jnp.float32),
        "col",
        scatter_dimension=0,
        tiled=True,
    )
    right_sum = lax.psum_scatter(
        jnp.einsum("ijc,ikc->kjc", grad_pair, left_full, preferred_element_type=jnp.float32),
        "row",
        scatter_dimension=0,
        tiled=True,
    )
    grad_left = jnp.transpose(left_sum, (1, 0, 2)).astype(jnp.bfloat16)
    grad_right = jnp.transpose(right_sum, (1, 0, 2)).astype(jnp.bfloat16)
    return (grad_left, grad_right, grad_gate, grad_weight)


def solution(mesh):
    return jax.shard_map(
        local,
        mesh=mesh,
        in_specs=(
            P("row", "col", None),
            P("col", "row", None),
            P("row", "col", None),
            P(),
            P("row", "col", None),
        ),
        out_specs=(P("row", "col", None), P("col", "row", None), P("row", "col", None), P()),
        check_vma=False,
    )
```

profile of v0, /device:TPU:6, one launch (start us, length us, event | category | flops | bytes accessed | tf_op | source)
XLA Modules:
  0.0 758.2 jit_solution(16006399201181075151)
XLA Ops:
  7.2 0.0 copy-start
  7.2 0.0 all-gather.5.cloned.1.call-start
  7.2 1.8 copy.17
  9.0 0.0 all-gather.5.cloned.1.call-update
  9.0 0.0 all-gather.3.cloned.1.call-start
  9.1 1.8 copy.16
  10.8 0.0 all-gather.3.cloned.1.call-update
  10.8 0.0 reduce-scatter.3.cloned.1.call-start
  10.9 64.2 %all-gather.5.cloned.1.call-done = bf16[32,512,128]{2,0,1:T(8,128)(2,1)} async-done(((bf16[32,32,128]{2,0,1:T(8,128)(2,1)}), bf16[32,512,128]{2,0,1:T(8,128)(2,1)}) %all-gather.5.cloned.1.call-update) | async-done | bytes 4194320 | tf_op jit(solution)/shard_map/all_gather | solution.py:8
  75.1 8.6 %copy.19 = bf16[32,512,128]{1,0,2:T(8,128)(2,1)} copy(bf16[32,512,128]{2,0,1:T(8,128)(2,1)} %all-gather.5.cloned.1.call-done) | data formatting | bytes 8388608 | tf_op jit(solution)/shard_map/all_gather | solution.py:8
  83.6 91.7 %all-gather.3.cloned.1.call-done = bf16[32,512,128]{2,0,1:T(8,128)(2,1)} async-done(((bf16[32,32,128]{2,0,1:T(8,128)(2,1)}), bf16[32,512,128]{2,0,1:T(8,128)(2,1)}) %all-gather.3.cloned.1.call-update) | async-done | bytes 4194320 | tf_op jit(solution)/shard_map/all_gather | solution.py:9
  175.4 8.6 %copy.18 = bf16[32,512,128]{1,0,2:T(8,128)(2,1)} copy(bf16[32,512,128]{2,0,1:T(8,128)(2,1)} %all-gather.3.cloned.1.call-done) | data formatting | bytes 8388608 | tf_op jit(solution)/shard_map/all_gather | solution.py:9
  184.0 0.0 copy-start.1
  184.0 0.0 copy-start.2
  184.0 4.7 fusion.15
  188.7 1.4 copy.20
  190.2 0.2 bitcast_reduce_fusion
  190.4 0.4 multiply_reduce_fusion.1
  190.8 0.0 copy-done
  190.8 0.0 copy-done.1
  190.8 0.0 copy-done.2
  190.8 0.8 fusion.14
  191.7 0.6 multiply_convert_fusion
  192.3 1.6 copy.24
  193.9 6.7 convolution_bitcast_fusion.1
  200.6 11.0 %copy.23 = f32[512,32,128]{2,1,0:T(8,128)} copy(f32[512,32,128]{0,1,2:T(8,128)} %convolution_bitcast_fusion.1) | data formatting | bytes 16777216 | tf_op jit(solution)/shard_map/ijc,jkc->kic/transpose | solution.py:37
  211.6 0.0 reduce-scatter.3.cloned.1.call-update
  211.6 0.0 reduce-scatter.5.cloned.1.call-start
  211.6 6.6 convolution_bitcast_fusion
  218.3 11.1 %copy.26 = f32[512,32,128]{2,1,0:T(8,128)} copy(f32[512,32,128]{0,1,2:T(8,128)} %convolution_bitcast_fusion) | data formatting | bytes 16777216 | tf_op jit(solution)/shard_map/ijc,ikc->kjc/transpose | solution.py:43
  229.4 0.0 reduce-scatter.5.cloned.1.call-update
  229.4 0.0 all-reduce.2.cloned.1.call-start
  229.5 1.2 fusion.3
  230.7 1.2 fusion.2
  231.9 0.0 all-reduce.2.cloned.1.call-update
  231.9 90.2 %reduce-scatter.3.cloned.1.call-done = f32[32,32,128]{2,1,0:T(8,128)} async-done(((f32[512,32,128]{2,1,0:T(8,128)}), f32[32,32,128]{2,1,0:T(8,128)}) %reduce-scatter.3.cloned.1.call-update) | async-done | bytes 524304 | tf_op jit(solution)/shard_map/reduce_scatter | solution.py:36
  322.1 1.1 convert_bitcast_fusion.1
  323.2 0.8 copy.27
  324.0 182.4 %reduce-scatter.5.cloned.1.call-done = f32[32,32,128]{2,1,0:T(8,128)} async-done(((f32[512,32,128]{2,1,0:T(8,128)}), f32[32,32,128]{2,1,0:T(8,128)}) %reduce-scatter.5.cloned.1.call-update) | async-done | bytes 524304 | tf_op jit(solution)/shard_map/reduce_scatter | solution.py:42
  506.3 1.1 convert_bitcast_fusion
  507.4 0.8 copy.28
  508.2 242.0 %all-reduce.2.cloned.1.call-done = f32[128,128]{1,0:T(8,128)} async-done(((f32[128,128]{1,0:T(8,128)}), f32[128,128]{1,0:T(8,128)}) %all-reduce.2.cloned.1.call-update) | async-done | bytes 65552 | tf_op jit(solution)/shard_map/psum | solution.py:29
  750.2 1.5 copy.30
  (3 shorter events, 0.0 us)
Async XLA Ops:
  7.2 183.6 %copy-start = (bf16[128,128]{1,0:T(8,128)(2,1)S(1)}, bf16[128,128]{1,0:T(8,128)(2,1)}, u32[]{:S(2)}) copy-start(bf16[128,128]{1,0:T(8,128)(2,1)} %param.8) | copy-start | bytes 98308
  7.2 67.9 %all-gather.5.cloned.1.call-start = ((), (), s32[]{:S(2)}) async-start(), calls=%async_computation.3 | async-start | bytes 4456448 | tf_op jit(solution)/shard_map/all_gather | solution.py:8
  9.0 166.4 %all-gather.3.cloned.1.call-start = ((), (), s32[]{:S(2)}) async-start(), calls=%async_computation.2 | async-start | bytes 4456448 | tf_op jit(solution)/shard_map/all_gather | solution.py:9
  10.8 311.2 %reduce-scatter.3.cloned.1.call-start = ((), (), s32[]{:S(2)}) async-start(), calls=%async_computation.4 | async-start | bytes 8912896 | tf_op jit(solution)/shard_map/reduce_scatter | solution.py:36
  184.0 6.8 copy-start.1
  184.0 6.8 copy-start.2
  211.6 294.8 %reduce-scatter.5.cloned.1.call-start = ((), (), s32[]{:S(2)}) async-start(), calls=%async_computation.5 | async-start | bytes 8912896 | tf_op jit(solution)/shard_map/reduce_scatter | solution.py:42
  229.4 520.7 %all-reduce.2.cloned.1.call-start = ((), (), s32[]{:S(2)}) async-start(), calls=%async_computation.6 | async-start | bytes 131072 | tf_op jit(solution)/shard_map/psum | solution.py:29
Sparse Core Ops, SparseCore 0:
  11.3 63.7 all-gather.4
  77.4 97.9 all-gather.2
  211.7 110.3 reduce-scatter.2
  324.5 181.8 reduce-scatter.4
  512.3 237.8 all-reduce.1
where the time goes:
time: 761 us; the launch traced here: 758 us
  waiting for transfers between devices  670 us (88%)
  local copies, waits for them, and re-layouts  49 us (6%)
  matrix products  21.3 us (3%)
  between operations  13.9 us (2%)
    psum x1, waiting for transfers between devices, local(): grad_weight = lax.psum(weight_terms, ('row', 'col'))  242 us
    reduce_scatter x1, waiting for transfers between devices, local(): lax.psum_scatter(jnp.einsum('ijc,ikc->kjc', grad_pair, left_full, preferr...  182 us
    all_gather x1, waiting for transfers between devices, local(): right_full = lax.all_gather(right_proj, 'row', axis=1, tiled=True)  91.7 us
    reduce_scatter x1, waiting for transfers between devices, local(): lax.psum_scatter(jnp.einsum('ijc,jkc->kic', grad_pair, right_full, prefer...  90.2 us
    all_gather x1, waiting for transfers between devices, local(): left_full = lax.all_gather(left_proj, 'col', axis=1, tiled=True)  64.2 us
  transfers between devices with their start and end apart: 5, of which 5 were waited for; matrix products, arithmetic and copies ran while one was open for 5% of the time, Pallas kernels for 0%

commit v1 on v0

v1 whole, which is shorter than its diff:
```python
import jax
import jax.numpy as jnp
from jax import lax
from jax.experimental import pallas as pl
from jax.experimental.pallas import tpu as pltpu
from jax.sharding import PartitionSpec as P

F32 = jnp.float32
BF16 = jnp.bfloat16
BOTH = ("row", "col")
PARAMS = pltpu.CompilerParams(vmem_limit_bytes=32 * 1024 * 1024)
NT = (((1,), (1,)), ((), ()))
TN = (((0,), (0,)), ((), ()))


def chunk_transpose(parts):
    lane = lax.broadcasted_iota(jnp.int32, parts[0].shape, 1)
    low = lane < 64
    even = (lane & 32) == 0
    turn = lambda x, by: pltpu.roll(x, by, 1)
    y0, y1, y2, y3 = parts
    a0 = jnp.where(low, y0, turn(y2, 64))
    a2 = jnp.where(low, turn(y0, 64), y2)
    a1 = jnp.where(low, y1, turn(y3, 64))
    a3 = jnp.where(low, turn(y1, 64), y3)
    return [
        jnp.where(even, a0, turn(a1, 32)),
        jnp.where(even, turn(a0, 96), a1),
        jnp.where(even, a2, turn(a3, 32)),
        jnp.where(even, turn(a2, 96), a3),
    ]


def pack_kernel(left_ref, right_ref, out_ref, slabs):
    for side, ref in enumerate((left_ref, right_ref)):
        for s in range(8):
            slab = ref[pl.ds(s * 128, 128), :].astype(F32)
            slabs[:, side * 8 + s, :] = slab.T
    out_ref[...] = slabs[...].astype(BF16)


def unpack_kernel(in_ref, left_ref, right_ref, slabs):
    slabs[...] = in_ref[...].astype(F32)
    for side, ref in enumerate((left_ref, right_ref)):
        for s in range(8):
            ref[pl.ds(s * 128, 128), :] = slabs[:, side * 8 + s, :].T.astype(BF16)


def pair_kernel(core_ref, own_ref, other_ref, a_ref, b_ref, out_ref, va, vb, nat, prod):
    core = core_ref[0]

    @pl.when(core == 0)
    def _():
        va[...] = own_ref[...].astype(F32)
        vb[...] = other_ref[...].astype(F32)

    @pl.when(core == 1)
    def _():
        vb[...] = own_ref[...].astype(F32)
        va[...] = other_ref[...].astype(F32)

    for g in range(4):
        for rc in range(4):
            parts = [va[pl.ds(4 * rc, 4), 4 * g + t].reshape(32, 128) for t in range(4)]
            for lo, part in enumerate(chunk_transpose(parts)):
                a_ref[pl.ds(lo * 128 + rc * 32, 32), pl.ds(g * 128, 128)] = part.astype(BF16)
            parts = [vb[4 * g + t, pl.ds(4 * rc, 4)].reshape(32, 128) for t in range(4)]
            for lo, part in enumerate(chunk_transpose(parts)):
                nat[g, pl.ds(rc * 128 + lo, 32, stride=4), :] = part
    for g in range(4):
        b_ref[:, pl.ds(g * 128, 128)] = nat[g].astype(BF16)
    for g in range(4):
        rows = pl.ds(g * 128, 128)
        prod[g] = lax.dot_general(a_ref[...], b_ref[rows, :], NT, preferred_element_type=F32)
    for half in range(2):

        @pl.when(core == half)
        def _():
            for g in range(4):
                for rc in range(4):
                    parts = [prod[g, pl.ds(lo * 128 + rc * 32, 32), :] for lo in range(4)]
                    for t, part in enumerate(chunk_transpose(parts)):
                        out_ref[pl.ds(4 * rc, 4), 4 * g + t] = part.reshape(4, 8, 128)[
                            :, 4 * half : 4 * half + 4
                        ]


def norm_kernel(pair_ref, gate_ref, grad_ref, weight_ref, gate_out, weight_out, out_ref, slabs):
    weight = weight_ref[...]
    total = jnp.zeros((128, 128), F32)
    for s in range(8):
        rows = pl.ds(s * 128, 128)
        pair = pair_ref[:, s, :].T
        average = jnp.mean(pair, axis=-1, keepdims=True)
        centered = pair - average
        variance = jnp.mean(centered * centered, axis=-1, keepdims=True)
        inv_std = lax.rsqrt(variance + 1e-05)
        normed = centered * inv_std
        normed_half = normed.astype(BF16)
        gate_prob = jax.nn.sigmoid(gate_ref[rows, :].astype(F32))
        upstream = grad_ref[rows, :].astype(F32)
        gated = upstream * gate_prob
        gated_grad = gated.astype(BF16)
        projected = jnp.dot(normed_half, weight, preferred_element_type=F32)
        gate_out[rows, :] = (gated * projected * (1.0 - gate_prob)).astype(BF16)
        total += lax.dot_general(normed_half, gated_grad, TN, preferred_element_type=F32)
        grad_normed = lax.dot_general(gated_grad, weight, NT, preferred_element_type=F32)
        mean_one = jnp.mean(grad_normed, axis=-1, keepdims=True)
        mean_two = jnp.mean(grad_normed * normed, axis=-1, keepdims=True)
        grad_pair = (grad_normed - mean_one - normed * mean_two) * inv_std
        slabs[:, s, :] = grad_pair.T
    weight_out[...] = total * (1.0 / 512.0)
    out_ref[...] = slabs[...].astype(BF16)


def grad_kernel(core_ref, own_ref, other_ref, a_ref, b_ref, out_ref, raw, gp, prod):
    core = core_ref[0]

    @pl.when(core == 0)
    def _():
        raw[:, :, 0:4, :] = own_ref[...].astype(F32)
        raw[:, :, 4:8, :] = other_ref[...].astype(F32)

    @pl.when(core == 1)
    def _():
        raw[:, :, 0:4, :] = other_ref[...].astype(F32)
        raw[:, :, 4:8, :] = own_ref[...].astype(F32)

    for g in range(4):
        for rc in range(4):
            parts = [raw[pl.ds(4 * rc, 4), 4 * g + t].reshape(32, 128) for t in range(4)]
            for lo, part in enumerate(chunk_transpose(parts)):
                gp[pl.ds(lo * 128 + rc * 32, 32), pl.ds(g * 128, 128)] = part.astype(BF16)

    @pl.when(core == 0)
    def _():
        for g in range(4):
            prod[g] = jnp.dot(gp[...], b_ref[:, pl.ds(g * 128, 128)], preferred_element_type=F32)
            for rc in range(4):
                parts = [prod[g, pl.ds(lo * 128 + rc * 32, 32), :] for lo in range(4)]
                for t, part in enumerate(chunk_transpose(parts)):
                    out_ref[pl.ds(4 * rc, 4), 4 * g + t] = part.reshape(4, 8, 128).astype(BF16)

    @pl.when(core == 1)
    def _():
        for g in range(4):
            prod[g] = lax.dot_general(
                gp[...], a_ref[:, pl.ds(g * 128, 128)], TN, preferred_element_type=F32
            )
            for qc in range(4):
                parts = [
                    prod[g, pl.ds(qc * 128 + lo, 32, stride=4), :] for lo in range(4)
                ]
                for t, part in enumerate(chunk_transpose(parts)):
                    out_ref[4 * g + t, pl.ds(4 * qc, 4)] = part.reshape(4, 8, 128).astype(BF16)


VM = pl.BlockSpec(memory_space=pltpu.VMEM)
SM = pl.BlockSpec(memory_space=pltpu.SMEM)


def call(kernel, outs, ins, scratch, name):
    return pl.pallas_call(
        kernel,
        out_shape=[jax.ShapeDtypeStruct(s, d) for s, d in outs],
        in_specs=ins,
        out_specs=[VM] * len(outs),
        scratch_shapes=[pltpu.VMEM(s, d) for s, d in scratch],
        compiler_params=PARAMS,
        name=name,
    )


def exchange(x, axis):
    return lax.all_to_all(x, axis, 0, 0, tiled=True)


def other_core(x):
    return lax.ppermute(x, "col", [(i, i ^ 1) for i in range(16)])


def local(left_proj, right_proj, gate, out_weight, grad_out):
    core = (lax.axis_index("col") % 2).astype(jnp.int32).reshape(1)
    (packed,) = call(pack_kernel, [((128, 16, 128), BF16)], [VM] * 2, [((128, 16, 128), F32)], "pack")(
        left_proj.reshape(1024, 128), right_proj.reshape(1024, 128)
    )
    own = exchange(packed.reshape(256, 8, 128), BOTH)
    other = other_core(own)
    block = (16, 16, 8, 128)
    a, b, pair = call(
        pair_kernel,
        [((512, 512), BF16), ((512, 512), BF16), ((16, 16, 4, 128), F32)],
        [SM, VM, VM],
        [(block, F32), (block, F32), ((4, 512, 128), F32), ((4, 512, 128), F32)],
        "pair",
    )(core, own.reshape(block), other.reshape(block))
    pair = exchange(pair.reshape(256, 4, 128), BOTH).reshape(128, 8, 128)
    grad_gate, weight_terms, grad_pair = call(
        norm_kernel,
        [((1024, 128), BF16), ((128, 128), F32), ((128, 8, 128), BF16)],
        [VM] * 4,
        [((128, 8, 128), F32)],
        "norm",
    )(pair, gate.reshape(1024, 128), grad_out.reshape(1024, 128), out_weight)
    own = exchange(grad_pair.reshape(256, 4, 128), BOTH)
    other = other_core(own)
    half = (16, 16, 4, 128)
    (grads,) = call(
        grad_kernel,
        [(block, BF16)],
        [SM, VM, VM, VM, VM],
        [(block, F32), ((512, 512), BF16), ((4, 512, 128), F32)],
        "grads",
    )(core, own.reshape(half), other.reshape(half), a, b)
    grads = exchange(grads.reshape(256, 8, 128), BOTH).reshape(128, 16, 128)
    grad_left, grad_right = call(
        unpack_kernel, [((1024, 128), BF16)] * 2, [VM], [((128, 16, 128), F32)], "unpack"
    )(grads)
    part = exchange(weight_terms.reshape(16, 8, 128), "col").sum(0)
    part = exchange(jnp.broadcast_to(part[None], (16, 8, 128)), "row").sum(0)
    grad_weight = exchange(jnp.broadcast_to(part[None], (16, 8, 128)), "col").reshape(128, 128)
    shape = (32, 32, 128)
    return grad_left.reshape(shape), grad_right.reshape(shape), grad_gate.reshape(shape), grad_weight


def solution(mesh):
    return jax.shard_map(
        local,
        mesh=mesh,
        in_specs=(
            P("row", "col", None),
            P("col", "row", None),
            P("row", "col", None),
            P(),
            P("row", "col", None),
        ),
        out_specs=(P("row", "col", None), P("col", "row", None), P("row", "col", None), P()),
        check_vma=False,
    )
```

time: 761 us -> 160 us (0.21)
  the two profiles are of different devices: /device:TPU:6 before, /device:TPU:1 now
where the time goes in v1:
time: 160 us; the launch traced here: 159 us
  blocking collectives  105 us (66%)
  waiting for transfers between devices  26.9 us (17%)
  Pallas kernels  12.8 us (8%)
  starting transfers between devices  10.4 us (6%)
  local copies, waits for them, and re-layouts  3.19 us (2%)
    all_to_all x5, blocking collectives, exchange(): return lax.all_to_all(x, axis, 0, 0, tiled=True)  105 us
    all_to_all x2, waiting for transfers between devices, exchange(): return lax.all_to_all(x, axis, 0, 0, tiled=True)  25 us
    all_to_all x2, starting transfers between devices, exchange(): return lax.all_to_all(x, axis, 0, 0, tiled=True)  10.4 us
    pallas_call x1, Pallas kernels, local(): call(grad_kernel, [(block, BF16)], [SM, VM, VM, VM, VM], [(block, F32), (...  4.06 us
    pallas_call x1, Pallas kernels, local(): call(pair_kernel, [((512, 512), BF16), ((512, 512), BF16), ((16, 16, 4, 1...  3.67 us
  transfers between devices with their start and end apart: 4, of which 3 were waited for; matrix products, arithmetic and copies ran while one was open for 0% of the time, Pallas kernels for 3%

profile of v1, /device:TPU:1, one launch (start us, length us, event | category | flops | bytes accessed | tf_op | source)
XLA Modules:
  0.0 159.2 jit_solution(852215735430014762)
XLA Ops:
  0.6 0.0 copy-start
  0.6 0.9 copy-done
  1.6 0.0 copy-start.1
  1.6 0.9 copy-done.1
  2.5 0.7 pack.1
  3.3 36.9 %all_to_all.35 = bf16[256,8,128]{2,1,0:T(8,128)(2,1)S(1)} all-to-all(bf16[256,8,128]{2,1,0:T(8,128)(2,1)S(1)} %bitcast.23), channel_id=1, replica_groups=mesh['row'=16,'col'=16] {'row','col'}, dimensions={0} | all-to-all | bytes 1048576 | tf_op jit(solution)/shard_map/all_to_all | solution.py:175
  40.2 0.0 collective-permute-start
  40.2 1.9 %collective-permute-done = bf16[256,8,128]{2,1,0:T(8,128)(2,1)S(1)} collective-permute-done((bf16[256,8,128]{2,1,0:T(8,128)(2,1)S(1)}, bf16[256,8,128]{2,1,0:T(8,128)(2,1)S(1)}, u32[]{:S(2)}, u32[]{:S(2)}) %collective-permute-start) | collective-permute-done | bytes 524320 | tf_op jit(solution)/shard_map/ppermute | solution.py:179
  42.1 3.7 %pair.1 = (bf16[512,512]{1,0:T(8,128)(2,1)S(1)}, bf16[512,512]{1,0:T(8,128)(2,1)S(1)}, f32[16,16,4,128]{3,2,1,0:T(4,128)S(1)}) custom-call(s32[1]{0:T(128)} %bitcast.core_ref, bf16[16,16,8,128]{3,2,1,0:T(8,128)(2,1)S(1)} %bitcast.20, bf16[16,16,8,128]{3,2,1,0:T(8,128)(2,1)S(1)} %bitcast.26), custom_call_target="tpu_custom_call" | custom-call | tf_op jit(solution)/shard_map/pair/pallas_call | solution.py:190
  45.8 0.0 copy-start.2
  45.8 0.0 copy-start.3
  45.8 0.0 copy-start.4
  45.8 26.6 %all_to_all.36 = f32[256,4,128]{2,1,0:T(4,128)S(1)} all-to-all(f32[256,4,128]{2,1,0:T(4,128)S(1)} %bitcast.25), channel_id=1, replica_groups=mesh['row'=16,'col'=16] {'row','col'}, dimensions={0} | all-to-all | bytes 1048576 | tf_op jit(solution)/shard_map/all_to_all | solution.py:175
  72.4 0.0 copy-done.2
  72.4 0.0 copy-done.3
  72.4 0.0 copy-done.4
  72.4 3.0 %norm.1 = (bf16[1024,128]{1,0:T(8,128)(2,1)}, f32[128,128]{1,0:T(8,128)S(1)}, bf16[128,8,128]{2,1,0:T(8,128)(2,1)S(1)}) custom-call(f32[128,8,128]{2,1,0:T(8,128)S(1)} %bitcast.22, bf16[1024,128]{1,0:T(8,128)(2,1)S(1)} %bitcast.31, bf16[1024,128]{1,0:T(8,128)(2,1)S(1)} %bitcast.32, bf16[128,128]{1,0:T(8,128)(2,1)S(1)} %copy-done.4), custom_call_target="tpu_custom_call" | custom-call | tf_op jit(solution)/shard_map/norm/pallas_call | solution.py:198
  75.4 20.4 %all_to_all.37 = bf16[256,4,128]{2,1,0:T(4,128)(2,1)S(1)} all-to-all(bf16[256,4,128]{2,1,0:T(4,128)(2,1)S(1)} %bitcast.28), channel_id=1, replica_groups=mesh['row'=16,'col'=16] {'row','col'}, dimensions={0} | all-to-all | bytes 524288 | tf_op jit(solution)/shard_map/all_to_all | solution.py:175
  95.7 0.0 collective-permute-start.1
  95.7 10.7 %all_to_all.38 = f32[16,8,128]{2,1,0:T(8,128)S(1)} all-to-all(f32[16,8,128]{2,1,0:T(8,128)S(1)} %bitcast.33), channel_id=1, replica_groups=mesh['row'=16,'col'=16] {'col'}, dimensions={0} | all-to-all | bytes 131072 | tf_op jit(solution)/shard_map/all_to_all | solution.py:175
  106.5 10.5 %all_to_all.39 = f32[16,8,128]{2,1,0:T(8,128)S(1)} all-to-all(f32[16,8,128]{2,1,0:T(8,128)S(1)} %broadcast_in_dim.4), channel_id=1, replica_groups=mesh['row'=16,'col'=16] {'row'}, dimensions={0} | all-to-all | bytes 131072 | tf_op jit(solution)/shard_map/all_to_all | solution.py:175
  117.0 0.6 broadcast_in_dim.5
  117.7 5.0 %all-to-all-start.6 = ((f32[16,8,128]{2,1,0:T(8,128)}), f32[16,8,128]{2,1,0:T(8,128)S(1)}, u32[]{:S(2)}, u32[]{:S(2)}) async-start(f32[16,8,128]{2,1,0:T(8,128)} %broadcast_in_dim.5), calls=%async_computation.6 | async-start | bytes 131072 | tf_op jit(solution)/shard_map/all_to_all | solution.py:175
  122.7 0.0 collective-permute-done.1
  122.7 4.1 %grads.1 = bf16[16,16,8,128]{3,2,1,0:T(8,128)(2,1)} custom-call(s32[1]{0:T(128)} %bitcast.core_ref, bf16[16,16,4,128]{3,2,1,0:T(4,128)(2,1)S(1)} %bitcast.24, bf16[16,16,4,128]{3,2,1,0:T(4,128)(2,1)S(1)} %bitcast.27, bf16[512,512]{1,0:T(8,128)(2,1)S(1)} %get-tuple-element.14.a_ref, bf16[512,512]{1,0:T(8,128)(2,1)S(1)} %get-tuple-element.15.b_ref), custom_call_target="tpu_custom_call" | custom-call | tf_op jit(solution)/shard_map/grads/pallas_call | solution.py:208
  126.7 3.4 %all-to-all-done.6 = f32[16,8,128]{2,1,0:T(8,128)S(1)} async-done(((f32[16,8,128]{2,1,0:T(8,128)}), f32[16,8,128]{2,1,0:T(8,128)S(1)}, u32[]{:S(2)}, u32[]{:S(2)}) %all-to-all-start.6) | async-done | bytes 65568 | tf_op jit(solution)/shard_map/all_to_all | solution.py:175
  130.1 5.4 %all-to-all-start.3 = ((bf16[256,8,128]{2,1,0:T(8,128)(2,1)}), bf16[256,8,128]{2,1,0:T(8,128)(2,1)S(1)}, u32[]{:S(2)}, u32[]{:S(2)}) async-start(bf16[256,8,128]{2,1,0:T(8,128)(2,1)} %bitcast.13), calls=%async_computation.3 | async-start | bytes 1048576 | tf_op jit(solution)/shard_map/all_to_all | solution.py:175
  135.5 21.6 %all-to-all-done.3 = bf16[256,8,128]{2,1,0:T(8,128)(2,1)S(1)} async-done(((bf16[256,8,128]{2,1,0:T(8,128)(2,1)}), bf16[256,8,128]{2,1,0:T(8,128)(2,1)S(1)}, u32[]{:S(2)}, u32[]{:S(2)}) %all-to-all-start.3) | async-done | bytes 524320 | tf_op jit(solution)/shard_map/all_to_all | solution.py:175
  157.1 1.4 unpack.1
  158.5 0.6 copy.10
  (3 shorter events, 0.0 us)
Async XLA Ops:
  0.6 1.0 copy-start
  1.6 0.9 copy-start.1
  40.2 1.9 %collective-permute-start = (bf16[256,8,128]{2,1,0:T(8,128)(2,1)S(1)}, bf16[256,8,128]{2,1,0:T(8,128)(2,1)S(1)}, u32[]{:S(2)}, u32[]{:S(2)}) collective-permute-start(bf16[256,8,128]{2,1,0:T(8,128)(2,1)S(1)} %all_to_all.35), channel_id=1, source_target_pairs={{0,1},{1,0},{2,3},{3,2},{4,5},{5,4},{6,7},{7,6},{8,9},{9,8},{10,11... | collective-permute-start | bytes 1572872 | tf_op jit(solution)/shard_map/ppermute | solution.py:179
  45.8 26.6 %copy-start.2 = (bf16[32,32,128]{2,1,0:T(8,128)(2,1)S(1)}, bf16[32,32,128]{2,1,0:T(8,128)(2,1)}, u32[]{:S(2)}) copy-start(bf16[32,32,128]{2,1,0:T(8,128)(2,1)} %param.7) | copy-start | bytes 786436
  45.8 26.6 %copy-start.3 = (bf16[32,32,128]{2,1,0:T(8,128)(2,1)S(1)}, bf16[32,32,128]{2,1,0:T(8,128)(2,1)}, u32[]{:S(2)}) copy-start(bf16[32,32,128]{2,1,0:T(8,128)(2,1)} %param.9) | copy-start | bytes 786436
  45.8 26.6 %copy-start.4 = (bf16[128,128]{1,0:T(8,128)(2,1)S(1)}, bf16[128,128]{1,0:T(8,128)(2,1)}, u32[]{:S(2)}) copy-start(bf16[128,128]{1,0:T(8,128)(2,1)} %weight_ref.1) | copy-start | bytes 98308
  95.7 26.9 %collective-permute-start.1 = (bf16[256,4,128]{2,1,0:T(4,128)(2,1)S(1)}, bf16[256,4,128]{2,1,0:T(4,128)(2,1)S(1)}, u32[]{:S(2)}, u32[]{:S(2)}) collective-permute-start(bf16[256,4,128]{2,1,0:T(4,128)(2,1)S(1)} %all_to_all.37), channel_id=1, source_target_pairs={{0,1},{1,0},{2,3},{3,2},{4,5},{5,4},{6,7},{7,6},{8,9},{9,8},{10,11... | collective-permute-start | bytes 786440 | tf_op jit(solution)/shard_map/ppermute | solution.py:179
  117.7 12.4 %all-to-all-start.6 = ((f32[16,8,128]{2,1,0:T(8,128)}), f32[16,8,128]{2,1,0:T(8,128)S(1)}, u32[]{:S(2)}, u32[]{:S(2)}) async-start(f32[16,8,128]{2,1,0:T(8,128)} %broadcast_in_dim.5), calls=%async_computation.6 | async-start | bytes 131072 | tf_op jit(solution)/shard_map/all_to_all | solution.py:175
  130.1 27.0 %all-to-all-start.3 = ((bf16[256,8,128]{2,1,0:T(8,128)(2,1)}), bf16[256,8,128]{2,1,0:T(8,128)(2,1)S(1)}, u32[]{:S(2)}, u32[]{:S(2)}) async-start(bf16[256,8,128]{2,1,0:T(8,128)(2,1)} %bitcast.13), calls=%async_computation.3 | async-start | bytes 1048576 | tf_op jit(solution)/shard_map/all_to_all | solution.py:175

commit v2 on v1

--- a/solution.py
+++ b/solution.py
@@ -39,11 +39,18 @@
     out_ref[...] = slabs[...].astype(BF16)
 
 
-def unpack_kernel(in_ref, left_ref, right_ref, slabs):
-    slabs[...] = in_ref[...].astype(F32)
+def split_halves(x):
+    high = x.astype(BF16).astype(F32)
+    return high, (x - high).astype(BF16).astype(F32)
+
+
+def unpack_kernel(in_ref, left_ref, right_ref, weight_ref, slabs):
     for side, ref in enumerate((left_ref, right_ref)):
+        for pair in range(5):
+            slabs[:, 2 * pair : 2 * pair + 2, :] = in_ref[:, side, pair].astype(F32)
         for s in range(8):
-            ref[pl.ds(s * 128, 128), :] = slabs[:, side * 8 + s, :].T.astype(BF16)
+            ref[pl.ds(s * 128, 128), :] = slabs[:, s, :].T.astype(BF16)
+    weight_ref[...] = slabs[:, 8, :] + slabs[:, 9, :]
 
 
 def pair_kernel(core_ref, own_ref, other_ref, a_ref, b_ref, out_ref, va, vb, nat, prod):
@@ -85,7 +92,7 @@
                         ]
 
 
-def norm_kernel(pair_ref, gate_ref, grad_ref, weight_ref, gate_out, weight_out, out_ref, slabs):
+def norm_kernel(pair_ref, gate_ref, grad_ref, weight_ref, gate_out, out_ref, slabs):
     weight = weight_ref[...]
     total = jnp.zeros((128, 128), F32)
     for s in range(8):
@@ -109,8 +116,16 @@
         mean_two = jnp.mean(grad_normed * normed, axis=-1, keepdims=True)
         grad_pair = (grad_normed - mean_one - normed * mean_two) * inv_std
         slabs[:, s, :] = grad_pair.T
-    weight_out[...] = total * (1.0 / 512.0)
-    out_ref[...] = slabs[...].astype(BF16)
+    for half in range(2):
+        for pair in range(2):
+            at = 4 * half + 2 * pair
+            out_ref[:, half, pair] = slabs[:, at : at + 2, :].astype(BF16)
+    high, rest = split_halves(total * (1.0 / 512.0))
+    slabs[:, 0, :] = high
+    slabs[:, 1, :] = rest
+    terms = slabs[:, 0:2, :].astype(BF16)
+    out_ref[:, 0, 2] = terms
+    out_ref[:, 1, 2] = terms
 
 
 def grad_kernel(core_ref, own_ref, other_ref, a_ref, b_ref, out_ref, raw, gp, prod):
@@ -118,13 +133,20 @@
 
     @pl.when(core == 0)
     def _():
-        raw[:, :, 0:4, :] = own_ref[...].astype(F32)
-        raw[:, :, 4:8, :] = other_ref[...].astype(F32)
+        for pair in range(2):
+            raw[:, :, 2 * pair : 2 * pair + 2, :] = own_ref[:, :, pair].astype(F32)
+            raw[:, :, 4 + 2 * pair : 6 + 2 * pair, :] = other_ref[:, :, pair].astype(F32)
 
     @pl.when(core == 1)
     def _():
-        raw[:, :, 0:4, :] = other_ref[...].astype(F32)
-        raw[:, :, 4:8, :] = own_ref[...].astype(F32)
+        for pair in range(2):
+            raw[:, :, 2 * pair : 2 * pair + 2, :] = other_ref[:, :, pair].astype(F32)
+            raw[:, :, 4 + 2 * pair : 6 + 2 * pair, :] = own_ref[:, :, pair].astype(F32)
+
+    total = jnp.sum(own_ref[:, :, 2].astype(F32).reshape(256, 2, 128), axis=0)
+    high, rest = split_halves(jnp.sum(total, axis=0, keepdims=True))
+    terms = jnp.concatenate([high, rest], axis=0).astype(BF16)
+    out_ref[:, :, 4] = jnp.broadcast_to(terms[None, None], (16, 16, 2, 128))
 
     for g in range(4):
         for rc in range(4):
@@ -139,7 +161,11 @@
             for rc in range(4):
                 parts = [prod[g, pl.ds(lo * 128 + rc * 32, 32), :] for lo in range(4)]
                 for t, part in enumerate(chunk_transpose(parts)):
-                    out_ref[pl.ds(4 * rc, 4), 4 * g + t] = part.reshape(4, 8, 128).astype(BF16)
+                    block = part.reshape(4, 8, 128)
+                    for pair in range(4):
+                        out_ref[pl.ds(4 * rc, 4), 4 * g + t, pair] = block[
+                            :, 2 * pair : 2 * pair + 2
+                        ].astype(BF16)
 
     @pl.when(core == 1)
     def _():
@@ -152,7 +178,11 @@
                     prod[g, pl.ds(qc * 128 + lo, 32, stride=4), :] for lo in range(4)
                 ]
                 for t, part in enumerate(chunk_transpose(parts)):
-                    out_ref[4 * g + t, pl.ds(4 * qc, 4)] = part.reshape(4, 8, 128).astype(BF16)
+                    block = part.reshape(4, 8, 128)
+                    for pair in range(4):
+                        out_ref[4 * g + t, pl.ds(4 * qc, 4), pair] = block[
+                            :, 2 * pair : 2 * pair + 2
+                        ].astype(BF16)
 
 
 VM = pl.BlockSpec(memory_space=pltpu.VMEM)
@@ -195,30 +225,31 @@
         "pair",
     )(core, own.reshape(block), other.reshape(block))
     pair = exchange(pair.reshape(256, 4, 128), BOTH).reshape(128, 8, 128)
-    grad_gate, weight_terms, grad_pair = call(
+    grad_gate, grad_pair = call(
         norm_kernel,
-        [((1024, 128), BF16), ((128, 128), F32), ((128, 8, 128), BF16)],
+        [((1024, 128), BF16), ((128, 2, 3, 2, 128), BF16)],
         [VM] * 4,
         [((128, 8, 128), F32)],
         "norm",
     )(pair, gate.reshape(1024, 128), grad_out.reshape(1024, 128), out_weight)
-    own = exchange(grad_pair.reshape(256, 4, 128), BOTH)
+    own = exchange(grad_pair.reshape(256, 3, 2, 128), BOTH)
     other = other_core(own)
-    half = (16, 16, 4, 128)
+    half = (16, 16, 3, 2, 128)
     (grads,) = call(
         grad_kernel,
-        [(block, BF16)],
+        [((16, 16, 5, 2, 128), BF16)],
         [SM, VM, VM, VM, VM],
         [(block, F32), ((512, 512), BF16), ((4, 512, 128), F32)],
         "grads",
     )(core, own.reshape(half), other.reshape(half), a, b)
-    grads = exchange(grads.reshape(256, 8, 128), BOTH).reshape(128, 16, 128)
-    grad_left, grad_right = call(
-        unpack_kernel, [((1024, 128), BF16)] * 2, [VM], [((128, 16, 128), F32)], "unpack"
+    grads = exchange(grads.reshape(256, 5, 2, 128), BOTH).reshape(128, 2, 5, 2, 128)
+    grad_left, grad_right, grad_weight = call(
+        unpack_kernel,
+        [((1024, 128), BF16), ((1024, 128), BF16), ((128, 128), F32)],
+        [VM],
+        [((128, 10, 128), F32)],
+        "unpack",
     )(grads)
-    part = exchange(weight_terms.reshape(16, 8, 128), "col").sum(0)
-    part = exchange(jnp.broadcast_to(part[None], (16, 8, 128)), "row").sum(0)
-    grad_weight = exchange(jnp.broadcast_to(part[None], (16, 8, 128)), "col").reshape(128, 128)
     shape = (32, 32, 128)
     return grad_left.reshape(shape), grad_right.reshape(shape), grad_gate.reshape(shape), grad_weight
 

time: 160 us -> 134 us (0.84)
  waiting for transfers between devices: 26.9 us -> 3.63 us
  starting transfers between devices: 10.4 us -> 0.01 us
  blocking collectives: 105 us -> 115 us
    all_to_all x2 -> x0, waiting for transfers between devices: 25 us -> none  [exchange(): return lax.all_to_all(x, axis, 0, 0, tiled=True)]
    all_to_all x2 -> x0, starting transfers between devices: 10.4 us -> none  [exchange(): return lax.all_to_all(x, axis, 0, 0, tiled=True)]
    all_to_all x5 -> x4, blocking collectives: 105 us -> 115 us  [exchange(): return lax.all_to_all(x, axis, 0, 0, tiled=True)]
    ppermute x2, waiting for transfers between devices: 1.91 us -> 3.63 us  [other_core(): return lax.ppermute(x, 'col', [(i, i ^ 1) for i in range(16)])]
  transfers between devices with their start and end apart: 4 -> 2, of which waited for: 3 -> 2; matrix products, arithmetic and copies ran while one was open for 0% -> 0% of each run, Pallas kernels for 3% -> 0%
where the time goes in v2:
time: 134 us
  blocking collectives  115 us (86%)
  Pallas kernels  12.7 us (9%)
  waiting for transfers between devices  3.63 us (3%)
  local copies, waits for them, and re-layouts  1.91 us (1%)
    all_to_all x4, blocking collectives, exchange(): return lax.all_to_all(x, axis, 0, 0, tiled=True)  115 us
    pallas_call x1, Pallas kernels, local(): call(pair_kernel, [((512, 512), BF16), ((512, 512), BF16), ((16, 16, 4, 1...  3.69 us
    ppermute x2, waiting for transfers between devices, other_core(): return lax.ppermute(x, 'col', [(i, i ^ 1) for i in range(16)])  3.63 us
    pallas_call x1, Pallas kernels, local(): call(grad_kernel, [((16, 16, 5, 2, 128), BF16)], [SM, VM, VM, VM, VM], [(...  3.6 us
    pallas_call x1, Pallas kernels, local(): call(norm_kernel, [((1024, 128), BF16), ((128, 2, 3, 2, 128), BF16)], [VM...  2.95 us
  transfers between devices with their start and end apart: 2, of which 2 were waited for; matrix products, arithmetic and copies ran while one was open for 0% of the time, Pallas kernels for 0%

profile of v2, /device:TPU:1, one launch (start us, length us, event | category | flops | bytes accessed | tf_op | source)
XLA Modules:
  0.0 134.1 jit_solution(6390780257897921343)
XLA Ops:
  0.6 0.0 copy-start
  0.6 0.9 copy-done
  1.6 0.0 copy-start.1
  1.6 0.9 copy-done.1
  2.5 0.7 pack.1
  3.3 36.9 %all_to_all.20 = bf16[256,8,128]{2,1,0:T(8,128)(2,1)S(1)} all-to-all(bf16[256,8,128]{2,1,0:T(8,128)(2,1)S(1)} %bitcast.22), channel_id=1, replica_groups=mesh['row'=16,'col'=16] {'row','col'}, dimensions={0} | all-to-all | bytes 1048576 | tf_op jit(solution)/shard_map/all_to_all | solution.py:205
  40.2 0.0 collective-permute-start
  40.2 1.9 %collective-permute-done = bf16[256,8,128]{2,1,0:T(8,128)(2,1)S(1)} collective-permute-done((bf16[256,8,128]{2,1,0:T(8,128)(2,1)S(1)}, bf16[256,8,128]{2,1,0:T(8,128)(2,1)S(1)}, u32[]{:S(2)}, u32[]{:S(2)}) %collective-permute-start) | collective-permute-done | bytes 524320 | tf_op jit(solution)/shard_map/ppermute | solution.py:209
  42.1 3.7 %pair.1 = (bf16[512,512]{1,0:T(8,128)(2,1)S(1)}, bf16[512,512]{1,0:T(8,128)(2,1)S(1)}, f32[16,16,4,128]{3,2,1,0:T(4,128)S(1)}) custom-call(s32[1]{0:T(128)} %bitcast.core_ref, bf16[16,16,8,128]{3,2,1,0:T(8,128)(2,1)S(1)} %bitcast.20, bf16[16,16,8,128]{3,2,1,0:T(8,128)(2,1)S(1)} %bitcast.25), custom_call_target="tpu_custom_call" | custom-call | tf_op jit(solution)/shard_map/pair/pallas_call | solution.py:220
  45.8 0.0 copy-start.2
  45.8 0.0 copy-start.3
  45.8 0.0 copy-start.4
  45.8 26.6 %all_to_all.21 = f32[256,4,128]{2,1,0:T(4,128)S(1)} all-to-all(f32[256,4,128]{2,1,0:T(4,128)S(1)} %bitcast.24), channel_id=1, replica_groups=mesh['row'=16,'col'=16] {'row','col'}, dimensions={0} | all-to-all | bytes 1048576 | tf_op jit(solution)/shard_map/all_to_all | solution.py:205
  72.4 0.0 copy-done.2
  72.4 0.0 copy-done.3
  72.4 0.0 copy-done.4
  72.4 3.0 %norm.1 = (bf16[1024,128]{1,0:T(8,128)(2,1)}, bf16[128,2,3,2,128]{4,3,2,1,0:T(2,128)(2,1)S(1)}) custom-call(f32[128,8,128]{2,1,0:T(8,128)S(1)} %bitcast.21, bf16[1024,128]{1,0:T(8,128)(2,1)S(1)} %bitcast.30, bf16[1024,128]{1,0:T(8,128)(2,1)S(1)} %bitcast.31, bf16[128,128]{1,0:T(8,128)(2,1)S(1)} %copy-done.4), custom_call_target="tpu_custom_call" | custom-call | tf_op jit(solution)/shard_map/norm/pallas_call | solution.py:228
  75.4 23.1 %all_to_all.22 = bf16[256,3,2,128]{3,2,1,0:T(2,128)(2,1)S(1)} all-to-all(bf16[256,3,2,128]{3,2,1,0:T(2,128)(2,1)S(1)} %bitcast.26), channel_id=1, replica_groups=mesh['row'=16,'col'=16] {'row','col'}, dimensions={0} | all-to-all | bytes 786432 | tf_op jit(solution)/shard_map/all_to_all | solution.py:205
  98.5 0.0 collective-permute-start.1
  98.5 1.7 %collective-permute-done.1 = bf16[256,3,2,128]{3,2,1,0:T(2,128)(2,1)S(1)} collective-permute-done((bf16[256,3,2,128]{3,2,1,0:T(2,128)(2,1)S(1)}, bf16[256,3,2,128]{3,2,1,0:T(2,128)(2,1)S(1)}, u32[]{:S(2)}, u32[]{:S(2)}) %collective-permute-start.1) | collective-permute-done | bytes 393248 | tf_op jit(solution)/shard_map/ppermute | solution.py:209
  100.2 3.6 %grads.1 = bf16[16,16,5,2,128]{4,3,2,1,0:T(2,128)(2,1)S(1)} custom-call(s32[1]{0:T(128)} %bitcast.core_ref, bf16[16,16,3,2,128]{4,3,2,1,0:T(2,128)(2,1)S(1)} %bitcast.23, bf16[16,16,3,2,128]{4,3,2,1,0:T(2,128)(2,1)S(1)} %bitcast.27, bf16[512,512]{1,0:T(8,128)(2,1)S(1)} %get-tuple-element.14.a_ref, bf16[512,512]{1,0:T(8,128)(2,1)S(1)} %get-tuple-element.15.b_ref), custom_call_target="tpu_custom_call" | custom-call | tf_op jit(solution)/shard_map/grads/pallas_call | solution.py:238
  103.8 28.5 %all_to_all.23 = bf16[256,5,2,128]{3,2,1,0:T(2,128)(2,1)S(1)} all-to-all(bf16[256,5,2,128]{3,2,1,0:T(2,128)(2,1)S(1)} %bitcast.19), channel_id=1, replica_groups=mesh['row'=16,'col'=16] {'row','col'}, dimensions={0} | all-to-all | bytes 1310720 | tf_op jit(solution)/shard_map/all_to_all | solution.py:205
  132.4 1.7 %unpack.1 = (bf16[1024,128]{1,0:T(8,128)(2,1)}, bf16[1024,128]{1,0:T(8,128)(2,1)}, f32[128,128]{1,0:T(8,128)}) custom-call(bf16[128,2,5,2,128]{4,3,2,1,0:T(2,128)(2,1)S(1)} %bitcast.18), custom_call_target="tpu_custom_call" | custom-call | tf_op jit(solution)/shard_map/unpack/pallas_call | solution.py:246
Async XLA Ops:
  0.6 1.0 copy-start
  1.6 0.9 copy-start.1
  40.2 1.9 %collective-permute-start = (bf16[256,8,128]{2,1,0:T(8,128)(2,1)S(1)}, bf16[256,8,128]{2,1,0:T(8,128)(2,1)S(1)}, u32[]{:S(2)}, u32[]{:S(2)}) collective-permute-start(bf16[256,8,128]{2,1,0:T(8,128)(2,1)S(1)} %all_to_all.20), channel_id=1, source_target_pairs={{0,1},{1,0},{2,3},{3,2},{4,5},{5,4},{6,7},{7,6},{8,9},{9,8},{10,11... | collective-permute-start | bytes 1572872 | tf_op jit(solution)/shard_map/ppermute | solution.py:209
  45.8 26.6 %copy-start.2 = (bf16[32,32,128]{2,1,0:T(8,128)(2,1)S(1)}, bf16[32,32,128]{2,1,0:T(8,128)(2,1)}, u32[]{:S(2)}) copy-start(bf16[32,32,128]{2,1,0:T(8,128)(2,1)} %param.7) | copy-start | bytes 786436
  45.8 26.6 %copy-start.3 = (bf16[32,32,128]{2,1,0:T(8,128)(2,1)S(1)}, bf16[32,32,128]{2,1,0:T(8,128)(2,1)}, u32[]{:S(2)}) copy-start(bf16[32,32,128]{2,1,0:T(8,128)(2,1)} %param.9) | copy-start | bytes 786436
  45.8 26.6 %copy-start.4 = (bf16[128,128]{1,0:T(8,128)(2,1)S(1)}, bf16[128,128]{1,0:T(8,128)(2,1)}, u32[]{:S(2)}) copy-start(bf16[128,128]{1,0:T(8,128)(2,1)} %weight_ref.1) | copy-start | bytes 98308
  98.5 1.7 %collective-permute-start.1 = (bf16[256,3,2,128]{3,2,1,0:T(2,128)(2,1)S(1)}, bf16[256,3,2,128]{3,2,1,0:T(2,128)(2,1)S(1)}, u32[]{:S(2)}, u32[]{:S(2)}) collective-permute-start(bf16[256,3,2,128]{3,2,1,0:T(2,128)(2,1)S(1)} %all_to_all.22), channel_id=1, source_target_pairs={{0,1},{1,0},{2,3},{3,2},{4,5},{5,4},{6,7},{7,6},{8,9},{9,8},{10,11... | collective-permute-start | bytes 1179656 | tf_op jit(solution)/shard_map/ppermute | solution.py:209

commit v3 on v1

v3 whole, which is shorter than its diff:
```python
import jax
import jax.numpy as jnp
from jax import lax
from jax.experimental import pallas as pl
from jax.experimental.pallas import tpu as pltpu
from jax.sharding import PartitionSpec as P

F32 = jnp.float32
BF16 = jnp.bfloat16
PARAMS = pltpu.CompilerParams(vmem_limit_bytes=32 * 1024 * 1024)
NT = (((1,), (1,)), ((), ()))
TN = (((0,), (0,)), ((), ()))

SAME_CORE = [[row * 16 + col for row in range(16) for col in range(core, 16, 2)] for core in (0, 1)]


def chunk_transpose(parts):
    lane = lax.broadcasted_iota(jnp.int32, parts[0].shape, 1)
    low = lane < 64
    even = (lane & 32) == 0
    turn = lambda x, by: pltpu.roll(x, by, 1)
    y0, y1, y2, y3 = parts
    a0 = jnp.where(low, y0, turn(y2, 64))
    a2 = jnp.where(low, turn(y0, 64), y2)
    a1 = jnp.where(low, y1, turn(y3, 64))
    a3 = jnp.where(low, turn(y1, 64), y3)
    return [
        jnp.where(even, a0, turn(a1, 32)),
        jnp.where(even, turn(a0, 96), a1),
        jnp.where(even, a2, turn(a3, 32)),
        jnp.where(even, turn(a2, 96), a3),
    ]


def split_halves(x):
    high = x.astype(BF16).astype(F32)
    return high, (x - high).astype(BF16).astype(F32)


def pack_kernel(core_ref, left_ref, right_ref, out_ref, slabs):
    for side, ref in enumerate((left_ref, right_ref)):
        for s in range(8):
            slab = ref[pl.ds(s * 128, 128), :].astype(F32)
            slabs[:, side * 8 + s, :] = slab.T
    out_ref[...] = slabs[...].astype(BF16)


def unpack_kernel(in_ref, left_ref, right_ref, weight_ref, slabs):
    slabs[...] = in_ref[...].astype(F32)
    for side, ref in enumerate((left_ref, right_ref)):
        for s in range(8):
            slab = slabs[pl.ds(side * 8 + s, 128, stride=18), :]
            ref[pl.ds(s * 128, 128), :] = slab.T.astype(BF16)
    weight_ref[...] = slabs[pl.ds(16, 128, stride=18), :] + slabs[pl.ds(17, 128, stride=18), :]


def order_kernel(core_ref, in_ref, a_ref, keep_ref, send_ref, raw, nat):
    core = core_ref[0]
    raw[...] = in_ref[...].astype(F32)
    for g in range(2):
        for rc in range(4):
            parts = [raw[pl.ds(4 * rc, 4), 4 * g + t, 0:8].reshape(32, 128) for t in range(4)]
            for lo, part in enumerate(chunk_transpose(parts)):
                a_ref[pl.ds(lo * 128 + rc * 32, 32), pl.ds(g * 128, 128)] = part.astype(BF16)
    for which, ref in enumerate((keep_ref, send_ref)):
        parity = core if which == 0 else 1 - core
        for g in range(2):
            for qc in range(2):
                parts = [
                    raw[2 * (4 * g + t) + parity, pl.ds(4 * qc, 4), 8:16].reshape(32, 128)
                    for t in range(4)
                ]
                for lo, part in enumerate(chunk_transpose(parts)):
                    nat[2 * which + g, pl.ds(qc * 128 + lo, 32, stride=4), :] = part
            ref[:, pl.ds(g * 128, 128)] = nat[2 * which + g].astype(BF16)


def pair_kernel(a_ref, other_ref, keep_ref, send_ref, out_ref, prod):
    value = lax.dot_general(a_ref[...], keep_ref[...], NT, preferred_element_type=F32)
    value += lax.dot_general(other_ref[...], send_ref[...], NT, preferred_element_type=F32)
    for g in range(2):
        prod[g] = value[:, g * 128 : (g + 1) * 128]
    for g in range(2):
        for rc in range(4):
            parts = [prod[g, pl.ds(lo * 128 + rc * 32, 32), :] for lo in range(4)]
            for t, part in enumerate(chunk_transpose(parts)):
                out_ref[pl.ds(4 * rc, 4), 4 * g + t] = part.reshape(4, 8, 128)


def norm_kernel(pair_ref, gate_ref, grad_ref, weight_ref, gate_out, out_ref, slabs):
    weight = weight_ref[...]
    total = jnp.zeros((128, 128), F32)
    for s in range(8):
        rows = pl.ds(s * 128, 128)
        pair = pair_ref[pl.ds(s, 128, stride=8), :]
        average = jnp.mean(pair, axis=0, keepdims=True)
        centered = pair - average
        variance = jnp.mean(centered * centered, axis=0, keepdims=True)
        inv_std = lax.rsqrt(variance + 1e-05)
        normed = centered * inv_std
        normed_half = normed.astype(BF16)
        gate_prob = jax.nn.sigmoid(gate_ref[rows, :].astype(F32))
        upstream = grad_ref[rows, :].astype(F32)
        gated = upstream * gate_prob
        gated_grad = gated.astype(BF16)
        projected = lax.dot_general(normed_half, weight, TN, preferred_element_type=F32)
        gate_out[rows, :] = (gated * projected * (1.0 - gate_prob)).astype(BF16)
        total += jnp.dot(normed_half, gated_grad, preferred_element_type=F32)
        grad_normed = lax.dot_general(weight, gated_grad, NT, preferred_element_type=F32)
        mean_one = jnp.mean(grad_normed, axis=0, keepdims=True)
        mean_two = jnp.mean(grad_normed * normed, axis=0, keepdims=True)
        grad_pair = (grad_normed - mean_one - normed * mean_two) * inv_std
        slabs[pl.ds(s, 128, stride=10), :] = grad_pair
    high, rest = split_halves(total * (1.0 / 512.0))
    slabs[pl.ds(8, 128, stride=10), :] = high
    slabs[pl.ds(9, 128, stride=10), :] = rest
    out_ref[...] = slabs[...].astype(BF16)


def grad_kernel(core_ref, own_ref, far_ref, a_ref, other_ref, keep_ref, got_ref, out_ref, raw, gp, prod, flat, out):
    core = core_ref[0]
    for which, ref in enumerate((own_ref, far_ref)):
        raw[which] = ref[...].astype(F32)
        for g in range(2):
            for rc in range(4):
                parts = [
                    jnp.concatenate(
                        [raw[which, pl.ds((8 * r + 4 * g + t) * 10, 8), :] for r in range(4 * rc, 4 * rc + 4)]
                    )
                    for t in range(4)
                ]
                for lo, part in enumerate(chunk_transpose(parts)):
                    gp[which, pl.ds(lo * 128 + rc * 32, 32), pl.ds(g * 128, 128)] = part.astype(BF16)

    terms = [raw[which, pl.ds(8 + row, 128, stride=10), :] for which in range(2) for row in range(2)]
    sums = [jnp.sum(term, axis=0, keepdims=True) for term in terms]
    high, rest = split_halves((sums[0] + sums[1]) + (sums[2] + sums[3]))
    out[pl.ds(16, 128, stride=18), :] = jnp.broadcast_to(high, (128, 128))
    out[pl.ds(17, 128, stride=18), :] = jnp.broadcast_to(rest, (128, 128))

    value = jnp.dot(gp[0], keep_ref[...], preferred_element_type=F32)
    value += jnp.dot(gp[1], got_ref[...], preferred_element_type=F32)
    for g in range(2):
        prod[g] = value[:, g * 128 : (g + 1) * 128]
    for g in range(2):
        for rc in range(4):
            parts = [prod[g, pl.ds(lo * 128 + rc * 32, 32), :] for lo in range(4)]
            for t, part in enumerate(chunk_transpose(parts)):
                for u in range(4):
                    first = ((4 * rc + u) * 8 + 4 * g + t) * 18
                    out[pl.ds(first, 8), :] = part[8 * u : 8 * u + 8]

    for which, ref in enumerate((a_ref, other_ref)):
        parity = core if which == 0 else 1 - core
        value = lax.dot_general(gp[0], ref[...], TN, preferred_element_type=F32)
        for g in range(2):
            flat[2 * which + g] = value[:, g * 128 : (g + 1) * 128]
        for g in range(2):
            for qc in range(2):
                parts = [
                    flat[2 * which + g, pl.ds(qc * 128 + lo, 32, stride=4), :] for lo in range(4)
                ]
                for t, part in enumerate(chunk_transpose(parts)):
                    for u in range(4):
                        first = parity * 144 + (4 * g + t) * 288 + (4 * qc + u) * 18 + 8
                        out[pl.ds(first, 8), :] = part[8 * u : 8 * u + 8]
    out_ref[...] = out[...].astype(BF16)


VM = pl.BlockSpec(memory_space=pltpu.VMEM)
SM = pl.BlockSpec(memory_space=pltpu.SMEM)


def call(kernel, outs, ins, scratch, name):
    return pl.pallas_call(
        kernel,
        out_shape=[jax.ShapeDtypeStruct(s, d) for s, d in outs],
        in_specs=ins,
        out_specs=[VM] * len(outs),
        scratch_shapes=[pltpu.VMEM(s, d) for s, d in scratch],
        compiler_params=PARAMS,
        name=name,
    )


def exchange(x):
    return lax.all_to_all(x, ("row", "col"), 0, 0, axis_index_groups=SAME_CORE, tiled=True)


def other_core(x):
    return lax.ppermute(x, "col", [(i, i ^ 1) for i in range(16)])


def local(left_proj, right_proj, gate, out_weight, grad_out):
    core = (lax.axis_index("col") & 1).astype(jnp.int32).reshape(1)
    (packed,) = call(pack_kernel, [((128, 16, 128), BF16)], [SM, VM, VM], [((128, 16, 128), F32)], "pack")(
        core, left_proj.reshape(1024, 128), right_proj.reshape(1024, 128)
    )
    blocks = exchange(packed)
    a, keep, send = call(
        order_kernel,
        [((512, 256), BF16), ((256, 256), BF16), ((256, 256), BF16)],
        [SM, VM],
        [((16, 8, 16, 128), F32), ((4, 256, 128), F32)],
        "order",
    )(core, blocks.reshape(16, 8, 16, 128))
    other = other_core(a)
    got = other_core(send)
    (pair,) = call(pair_kernel, [((16, 8, 8, 128), F32)], [VM] * 4, [((2, 512, 128), F32)], "pair")(
        a, other, keep, send
    )
    pair = exchange(pair.reshape(128, 8, 128))
    grad_gate, grad_pair = call(
        norm_kernel,
        [((1024, 128), BF16), ((1280, 128), BF16)],
        [VM] * 4,
        [((1280, 128), F32)],
        "norm",
    )(pair.reshape(1024, 128), gate.reshape(1024, 128), grad_out.reshape(1024, 128), out_weight)
    own = exchange(grad_pair.reshape(128, 5, 2, 128))
    far = other_core(own)
    (grads,) = call(
        grad_kernel,
        [((2304, 128), BF16)],
        [SM] + [VM] * 6,
        [
            ((2, 1280, 128), F32),
            ((2, 512, 256), BF16),
            ((2, 512, 128), F32),
            ((4, 256, 128), F32),
            ((2304, 128), F32),
        ],
        "grads",
    )(core, own.reshape(1280, 128), far.reshape(1280, 128), a, other, keep, got)
    grads = exchange(grads.reshape(128, 9, 2, 128))
    grad_left, grad_right, grad_weight = call(
        unpack_kernel,
        [((1024, 128), BF16), ((1024, 128), BF16), ((128, 128), F32)],
        [VM],
        [((2304, 128), F32)],
        "unpack",
    )(grads.reshape(2304, 128))
    shape = (32, 32, 128)
    return grad_left.reshape(shape), grad_right.reshape(shape), grad_gate.reshape(shape), grad_weight


def solution(mesh):
    return jax.shard_map(
        local,
        mesh=mesh,
        in_specs=(
            P("row", "col", None),
            P("col", "row", None),
            P("row", "col", None),
            P(),
            P("row", "col", None),
        ),
        out_specs=(P("row", "col", None), P("col", "row", None), P("row", "col", None), P()),
        check_vma=False,
    )
```

time: 160 us -> 124 us (0.78)
  the two profiles are of different devices: /device:TPU:1 before, /device:TPU:6 now
where the time goes in v3:
time: 124 us; the launch traced here: 123 us
  blocking collectives  110 us (89%)
  Pallas kernels  7.69 us (6%)
  waiting for transfers between devices  2.83 us (2%)
  local copies, waits for them, and re-layouts  1.91 us (2%)
    all_to_all x4, blocking collectives, exchange(): lax.all_to_all(x, ('row', 'col'), 0, 0, axis_index_groups=SAME_CORE, tile...  110 us
    pallas_call x1, Pallas kernels, local(): call(grad_kernel, [((2304, 128), BF16)], [SM] + [VM] * 6, [((2, 1280, 128...  3.03 us
    ppermute x3, waiting for transfers between devices, other_core(): return lax.ppermute(x, 'col', [(i, i ^ 1) for i in range(16)])  2.83 us
  transfers between devices with their start and end apart: 3, of which 2 were waited for; matrix products, arithmetic and copies ran while one was open for 0% of the time, Pallas kernels for 0%

profile of v3, /device:TPU:6, one launch (start us, length us, event | category | flops | bytes accessed | tf_op | source)
XLA Modules:
  0.0 123.3 jit_solution(8939937342819537102)
XLA Ops:
  0.6 0.0 copy-start
  0.6 0.9 copy-done
  1.6 0.0 copy-start.1
  1.6 0.9 copy-done.1
  2.5 0.7 pack.1
  3.3 34.7 %all_to_all.20 = bf16[128,16,128]{2,1,0:T(8,128)(2,1)S(1)} all-to-all(bf16[128,16,128]{2,1,0:T(8,128)(2,1)S(1)} %pack.1), channel_id=1, replica_groups={{0,2,4,6,8,10,12,14,16,18,20,22,24,26,28,30,32,34,36,38,40,42,44,46,48,..., dimensions={0} | all-to-all | bytes 1048576 | tf_op jit(solution)/shard_map/all_to_all | solution.py:187
  37.9 1.1 order.1
  39.1 0.1 collective-permute-start
  39.2 1.5 %collective-permute-done.other_ref = bf16[512,256]{1,0:T(8,128)(2,1)S(1)} collective-permute-done((bf16[512,256]{1,0:T(8,128)(2,1)S(1)}, bf16[512,256]{1,0:T(8,128)(2,1)S(1)}, u32[]{:S(2)}, u32[]{:S(2)}) %collective-permute-start) | collective-permute-done | bytes 262176 | tf_op jit(solution)/shard_map/ppermute | solution.py:191
  40.7 0.5 pair.1
  41.2 0.0 copy-start.2
  41.2 0.0 copy-start.3
  41.3 0.0 copy-start.4
  41.3 26.4 %all_to_all.21 = f32[128,8,128]{2,1,0:T(8,128)S(1)} all-to-all(f32[128,8,128]{2,1,0:T(8,128)S(1)} %bitcast.20), channel_id=1, replica_groups={{0,2,4,6,8,10,12,14,16,18,20,22,24,26,28,30,32,34,36,38,40,42,44,46,48,..., dimensions={0} | all-to-all | bytes 1048576 | tf_op jit(solution)/shard_map/all_to_all | solution.py:187
  67.7 0.0 copy-done.2
  67.7 0.0 copy-done.3
  67.7 0.0 copy-done.4
  67.7 1.3 %norm.1 = (bf16[1024,128]{1,0:T(8,128)(2,1)}, bf16[1280,128]{1,0:T(8,128)(2,1)S(1)}) custom-call(f32[1024,128]{1,0:T(8,128)S(1)} %bitcast.19, bf16[1024,128]{1,0:T(8,128)(2,1)S(1)} %bitcast.26, bf16[1024,128]{1,0:T(8,128)(2,1)S(1)} %bitcast.27, bf16[128,128]{1,0:T(8,128)(2,1)S(1)} %copy-done.4), custom_call_target="tpu_custom_call" | custom-call | tf_op jit(solution)/shard_map/norm/pallas_call | solution.py:213
  68.9 20.8 %all_to_all.22 = bf16[128,5,2,128]{3,2,1,0:T(2,128)(2,1)S(1)} all-to-all(bf16[128,5,2,128]{3,2,1,0:T(2,128)(2,1)S(1)} %bitcast.23), channel_id=1, replica_groups={{0,2,4,6,8,10,12,14,16,18,20,22,24,26,28,30,32,34,36,38,40,42,44,46,48,..., dimensions={0} | all-to-all | bytes 655360 | tf_op jit(solution)/shard_map/all_to_all | solution.py:187
  89.7 0.0 collective-permute-start.1
  89.7 0.5 collective-permute-start.2
  90.2 1.3 %collective-permute-done.2.got_ref = bf16[256,256]{1,0:T(8,128)(2,1)S(1)} collective-permute-done((bf16[256,256]{1,0:T(8,128)(2,1)S(1)}, bf16[256,256]{1,0:T(8,128)(2,1)S(1)}, u32[]{:S(2)}, u32[]{:S(2)}) %collective-permute-start.2) | collective-permute-done | bytes 131104 | tf_op jit(solution)/shard_map/ppermute | solution.py:191
  91.6 0.0 collective-permute-done.1
  91.6 3.0 %grads.1 = bf16[2304,128]{1,0:T(8,128)(2,1)S(1)} custom-call(s32[1]{0:T(128)} %bitcast.core_ref, bf16[1280,128]{1,0:T(8,128)(2,1)S(1)} %bitcast.21, bf16[1280,128]{1,0:T(8,128)(2,1)S(1)} %bitcast.22, bf16[512,256]{1,0:T(8,128)(2,1)S(1)} %get-tuple-element.12.a_ref, bf16[512,256]{1,0:T(8,128)(2,1)S(1)} %collective-permute-done.other_ref, ...), custom_call_target="tpu_custom_call" | custom-call | tf_op jit(solution)/shard_map/grads/pallas_call | solution.py:222
  94.6 27.7 %all_to_all.23 = bf16[128,9,2,128]{3,2,1,0:T(2,128)(2,1)S(1)} all-to-all(bf16[128,9,2,128]{3,2,1,0:T(2,128)(2,1)S(1)} %bitcast.16), channel_id=1, replica_groups={{0,2,4,6,8,10,12,14,16,18,20,22,24,26,28,30,32,34,36,38,40,42,44,46,48,..., dimensions={0} | all-to-all | bytes 1179648 | tf_op jit(solution)/shard_map/all_to_all | solution.py:187
  122.2 1.0 unpack.1
Async XLA Ops:
  0.6 1.0 copy-start
  1.6 0.9 copy-start.1
  39.1 1.6 %collective-permute-start = (bf16[512,256]{1,0:T(8,128)(2,1)S(1)}, bf16[512,256]{1,0:T(8,128)(2,1)S(1)}, u32[]{:S(2)}, u32[]{:S(2)}) collective-permute-start(bf16[512,256]{1,0:T(8,128)(2,1)S(1)} %get-tuple-element.12.a_ref), channel_id=1, source_target_pairs={{0,1},{1,0},{2,3},{3,2},{4,5},{5,4},{6,7},{7,6},{8,9},{9,8},{10,11... | collective-permute-start | bytes 786440 | tf_op jit(solution)/shard_map/ppermute | solution.py:191
  41.2 26.4 %copy-start.2 = (bf16[32,32,128]{2,1,0:T(8,128)(2,1)S(1)}, bf16[32,32,128]{2,1,0:T(8,128)(2,1)}, u32[]{:S(2)}) copy-start(bf16[32,32,128]{2,1,0:T(8,128)(2,1)} %param.7) | copy-start | bytes 786436
  41.2 26.4 %copy-start.3 = (bf16[32,32,128]{2,1,0:T(8,128)(2,1)S(1)}, bf16[32,32,128]{2,1,0:T(8,128)(2,1)}, u32[]{:S(2)}) copy-start(bf16[32,32,128]{2,1,0:T(8,128)(2,1)} %param.9) | copy-start | bytes 786436
  41.3 26.4 %copy-start.4 = (bf16[128,128]{1,0:T(8,128)(2,1)S(1)}, bf16[128,128]{1,0:T(8,128)(2,1)}, u32[]{:S(2)}) copy-start(bf16[128,128]{1,0:T(8,128)(2,1)} %weight_ref.1) | copy-start | bytes 98308
  89.7 1.8 %collective-permute-start.1 = (bf16[128,5,2,128]{3,2,1,0:T(2,128)(2,1)S(1)}, bf16[128,5,2,128]{3,2,1,0:T(2,128)(2,1)S(1)}, u32[]{:S(2)}, u32[]{:S(2)}) collective-permute-start(bf16[128,5,2,128]{3,2,1,0:T(2,128)(2,1)S(1)} %all_to_all.22), channel_id=1, source_target_pairs={{0,1},{1,0},{2,3},{3,2},{4,5},{5,4},{6,7},{7,6},{8,9},{9,8},{10,11... | collective-permute-start | bytes 983048 | tf_op jit(solution)/shard_map/ppermute | solution.py:191
  89.7 1.8 %collective-permute-start.2 = (bf16[256,256]{1,0:T(8,128)(2,1)S(1)}, bf16[256,256]{1,0:T(8,128)(2,1)S(1)}, u32[]{:S(2)}, u32[]{:S(2)}) collective-permute-start(bf16[256,256]{1,0:T(8,128)(2,1)S(1)} %get-tuple-element.14.send_ref), channel_id=1, source_target_pairs={{0,1},{1,0},{2,3},{3,2},{4,5},{5,4},{6,7},{7,6},{8,9},{9,8},{10,11... | collective-permute-start | bytes 393224 | tf_op jit(solution)/shard_map/ppermute | solution.py:191

commit v4 on v3

--- a/solution.py
+++ b/solution.py
@@ -37,10 +37,10 @@
     return high, (x - high).astype(BF16).astype(F32)
 
 
-def pack_kernel(core_ref, left_ref, right_ref, out_ref, slabs):
-    for side, ref in enumerate((left_ref, right_ref)):
+def pack_kernel(core_ref, in_ref, out_ref, slabs):
+    for side in range(2):
         for s in range(8):
-            slab = ref[pl.ds(s * 128, 128), :].astype(F32)
+            slab = in_ref[pl.ds(side * 1024 + s * 128, 128), :].astype(F32)
             slabs[:, side * 8 + s, :] = slab.T
     out_ref[...] = slabs[...].astype(BF16)
 
@@ -54,20 +54,24 @@
     weight_ref[...] = slabs[pl.ds(16, 128, stride=18), :] + slabs[pl.ds(17, 128, stride=18), :]
 
 
-def order_kernel(core_ref, in_ref, a_ref, keep_ref, send_ref, raw, nat):
-    core = core_ref[0]
-    raw[...] = in_ref[...].astype(F32)
-    for g in range(2):
-        for rc in range(4):
-            parts = [raw[pl.ds(4 * rc, 4), 4 * g + t, 0:8].reshape(32, 128) for t in range(4)]
+def left_order_kernel(in_ref, a_ref, raw):
+    raw[...] = in_ref[:, :, 0:8].astype(F32)
+    for g in range(2):
+        for rc in range(4):
+            parts = [raw[pl.ds(4 * rc, 4), 4 * g + t].reshape(32, 128) for t in range(4)]
             for lo, part in enumerate(chunk_transpose(parts)):
                 a_ref[pl.ds(lo * 128 + rc * 32, 32), pl.ds(g * 128, 128)] = part.astype(BF16)
+
+
+def right_order_kernel(core_ref, in_ref, keep_ref, send_ref, raw, nat):
+    core = core_ref[0]
+    raw[...] = in_ref[:, :, 8:16].astype(F32)
     for which, ref in enumerate((keep_ref, send_ref)):
         parity = core if which == 0 else 1 - core
         for g in range(2):
             for qc in range(2):
                 parts = [
-                    raw[2 * (4 * g + t) + parity, pl.ds(4 * qc, 4), 8:16].reshape(32, 128)
+                    raw[2 * (4 * g + t) + parity, pl.ds(4 * qc, 4)].reshape(32, 128)
                     for t in range(4)
                 ]
                 for lo, part in enumerate(chunk_transpose(parts)):
@@ -117,42 +121,29 @@
     out_ref[...] = slabs[...].astype(BF16)
 
 
-def grad_kernel(core_ref, own_ref, far_ref, a_ref, other_ref, keep_ref, got_ref, out_ref, raw, gp, prod, flat, out):
+def half_order(ref, raw, gp):
+    raw[...] = ref[...].astype(F32)
+    for g in range(2):
+        for rc in range(4):
+            parts = [
+                jnp.concatenate(
+                    [raw[pl.ds((8 * r + 4 * g + t) * 10, 8), :] for r in range(4 * rc, 4 * rc + 4)]
+                )
+                for t in range(4)
+            ]
+            for lo, part in enumerate(chunk_transpose(parts)):
+                gp[pl.ds(lo * 128 + rc * 32, 32), pl.ds(g * 128, 128)] = part.astype(BF16)
+    terms = [raw[pl.ds(8 + row, 128, stride=10), :] for row in range(2)]
+    return jnp.sum(terms[0], axis=0, keepdims=True) + jnp.sum(terms[1], axis=0, keepdims=True)
+
+
+def right_kernel(core_ref, own_ref, a_ref, other_ref, gp_ref, sum_ref, out_ref, raw, flat):
     core = core_ref[0]
-    for which, ref in enumerate((own_ref, far_ref)):
-        raw[which] = ref[...].astype(F32)
-        for g in range(2):
-            for rc in range(4):
-                parts = [
-                    jnp.concatenate(
-                        [raw[which, pl.ds((8 * r + 4 * g + t) * 10, 8), :] for r in range(4 * rc, 4 * rc + 4)]
-                    )
-                    for t in range(4)
-                ]
-                for lo, part in enumerate(chunk_transpose(parts)):
-                    gp[which, pl.ds(lo * 128 + rc * 32, 32), pl.ds(g * 128, 128)] = part.astype(BF16)
-
-    terms = [raw[which, pl.ds(8 + row, 128, stride=10), :] for which in range(2) for row in range(2)]
-    sums = [jnp.sum(term, axis=0, keepdims=True) for term in terms]
-    high, rest = split_halves((sums[0] + sums[1]) + (sums[2] + sums[3]))
-    out[pl.ds(16, 128, stride=18), :] = jnp.broadcast_to(high, (128, 128))
-    out[pl.ds(17, 128, stride=18), :] = jnp.broadcast_to(rest, (128, 128))
-
-    value = jnp.dot(gp[0], keep_ref[...], preferred_element_type=F32)
-    value += jnp.dot(gp[1], got_ref[...], preferred_element_type=F32)
-    for g in range(2):
-        prod[g] = value[:, g * 128 : (g + 1) * 128]
-    for g in range(2):
-        for rc in range(4):
-            parts = [prod[g, pl.ds(lo * 128 + rc * 32, 32), :] for lo in range(4)]
-            for t, part in enumerate(chunk_transpose(parts)):
-                for u in range(4):
-                    first = ((4 * rc + u) * 8 + 4 * g + t) * 18
-                    out[pl.ds(first, 8), :] = part[8 * u : 8 * u + 8]
-
+    sum_ref[...] = jnp.broadcast_to(half_order(own_ref, raw, gp_ref), (8, 128))
+    turned = gp_ref[...].T
     for which, ref in enumerate((a_ref, other_ref)):
         parity = core if which == 0 else 1 - core
-        value = lax.dot_general(gp[0], ref[...], TN, preferred_element_type=F32)
+        value = jnp.dot(turned, ref[...], preferred_element_type=F32)
         for g in range(2):
             flat[2 * which + g] = value[:, g * 128 : (g + 1) * 128]
         for g in range(2):
@@ -161,9 +152,27 @@
                     flat[2 * which + g, pl.ds(qc * 128 + lo, 32, stride=4), :] for lo in range(4)
                 ]
                 for t, part in enumerate(chunk_transpose(parts)):
-                    for u in range(4):
-                        first = parity * 144 + (4 * g + t) * 288 + (4 * qc + u) * 18 + 8
-                        out[pl.ds(first, 8), :] = part[8 * u : 8 * u + 8]
+                    where = (2 * (4 * g + t) + parity, pl.ds(4 * qc, 4))
+                    out_ref[where] = part.reshape(4, 8, 128).astype(BF16)
+
+
+def left_kernel(far_ref, gp_ref, keep_ref, got_ref, sum_ref, right_ref, out_ref, raw, gp, prod, out):
+    total = half_order(far_ref, raw, gp) + sum_ref[0:1, :]
+    high, rest = split_halves(total)
+    out[pl.ds(16, 128, stride=18), :] = jnp.broadcast_to(high, (128, 128))
+    out[pl.ds(17, 128, stride=18), :] = jnp.broadcast_to(rest, (128, 128))
+    value = jnp.dot(gp_ref[...], keep_ref[...], preferred_element_type=F32)
+    value += jnp.dot(gp[...], got_ref[...], preferred_element_type=F32)
+    for g in range(2):
+        prod[g] = value[:, g * 128 : (g + 1) * 128]
+    for g in range(2):
+        for rc in range(4):
+            parts = [prod[g, pl.ds(lo * 128 + rc * 32, 32), :] for lo in range(4)]
+            for t, part in enumerate(chunk_transpose(parts)):
+                for u in range(4):
+                    at = (4 * rc + u) * 8 + 4 * g + t
+                    out[pl.ds(at * 18, 8), :] = part[8 * u : 8 * u + 8]
+                    out[pl.ds(at * 18 + 8, 8), :] = right_ref[4 * rc + u, 4 * g + t].astype(F32)
     out_ref[...] = out[...].astype(BF16)
 
 
@@ -171,7 +180,7 @@
 SM = pl.BlockSpec(memory_space=pltpu.SMEM)
 
 
-def call(kernel, outs, ins, scratch, name):
+def call(kernel, outs, ins, scratch, name, us=1):
     return pl.pallas_call(
         kernel,
         out_shape=[jax.ShapeDtypeStruct(s, d) for s, d in outs],
@@ -179,6 +188,7 @@
         out_specs=[VM] * len(outs),
         scratch_shapes=[pltpu.VMEM(s, d) for s, d in scratch],
         compiler_params=PARAMS,
+        cost_estimate=pl.CostEstimate(flops=0, bytes_accessed=3_000_000 * us, transcendentals=0),
         name=name,
     )
 
@@ -193,22 +203,26 @@
 
 def local(left_proj, right_proj, gate, out_weight, grad_out):
     core = (lax.axis_index("col") & 1).astype(jnp.int32).reshape(1)
-    (packed,) = call(pack_kernel, [((128, 16, 128), BF16)], [SM, VM, VM], [((128, 16, 128), F32)], "pack")(
-        core, left_proj.reshape(1024, 128), right_proj.reshape(1024, 128)
-    )
-    blocks = exchange(packed)
-    a, keep, send = call(
-        order_kernel,
-        [((512, 256), BF16), ((256, 256), BF16), ((256, 256), BF16)],
+    sides = jnp.concatenate([left_proj.reshape(1024, 128), right_proj.reshape(1024, 128)])
+    (packed,) = call(
+        pack_kernel, [((128, 16, 128), BF16)], [SM, VM], [((128, 16, 128), F32)], "pack"
+    )(core, sides)
+    blocks = exchange(packed).reshape(16, 8, 16, 128)
+    (a,) = call(
+        left_order_kernel, [((512, 256), BF16)], [VM], [((16, 8, 8, 128), F32)], "left_order"
+    )(blocks)
+    other = other_core(a)
+    keep, send = call(
+        right_order_kernel,
+        [((256, 256), BF16), ((256, 256), BF16)],
         [SM, VM],
-        [((16, 8, 16, 128), F32), ((4, 256, 128), F32)],
-        "order",
-    )(core, blocks.reshape(16, 8, 16, 128))
-    other = other_core(a)
+        [((16, 8, 8, 128), F32), ((4, 256, 128), F32)],
+        "right_order",
+    )(core, blocks)
     got = other_core(send)
-    (pair,) = call(pair_kernel, [((16, 8, 8, 128), F32)], [VM] * 4, [((2, 512, 128), F32)], "pair")(
-        a, other, keep, send
-    )
+    (pair,) = call(
+        pair_kernel, [((16, 8, 8, 128), F32)], [VM] * 4, [((2, 512, 128), F32)], "pair"
+    )(a, other, keep, send)
     pair = exchange(pair.reshape(128, 8, 128))
     grad_gate, grad_pair = call(
         norm_kernel,
@@ -219,19 +233,20 @@
     )(pair.reshape(1024, 128), gate.reshape(1024, 128), grad_out.reshape(1024, 128), out_weight)
     own = exchange(grad_pair.reshape(128, 5, 2, 128))
     far = other_core(own)
+    half, total, right = call(
+        right_kernel,
+        [((512, 256), BF16), ((8, 128), F32), ((16, 8, 8, 128), BF16)],
+        [SM] + [VM] * 3,
+        [((1280, 128), F32), ((4, 256, 128), F32)],
+        "right",
+    )(core, own.reshape(1280, 128), a, other)
     (grads,) = call(
-        grad_kernel,
+        left_kernel,
         [((2304, 128), BF16)],
-        [SM] + [VM] * 6,
-        [
-            ((2, 1280, 128), F32),
-            ((2, 512, 256), BF16),
-            ((2, 512, 128), F32),
-            ((4, 256, 128), F32),
-            ((2304, 128), F32),
-        ],
-        "grads",
-    )(core, own.reshape(1280, 128), far.reshape(1280, 128), a, other, keep, got)
+        [VM] * 6,
+        [((1280, 128), F32), ((512, 256), BF16), ((2, 512, 128), F32), ((2304, 128), F32)],
+        "left",
+    )(far.reshape(1280, 128), half, keep, got, total, right)
     grads = exchange(grads.reshape(128, 9, 2, 128))
     grad_left, grad_right, grad_weight = call(
         unpack_kernel,

time: 124 us -> 120 us (0.968)
  local copies, waits for them, and re-layouts: 1.91 us -> 0.02 us
  waiting for transfers between devices: 2.83 us -> 1.13 us
    unnamed x10 -> x6, local copies, waits for them, and re-layouts: 1.91 us -> 0.02 us
    ppermute x3, waiting for transfers between devices: 2.83 us -> 1.13 us  [other_core(): return lax.ppermute(x, 'col', [(i, i ^ 1) for i in range(16)])]
    pallas_call x3 -> x5, Pallas kernels: 4.88 us -> 3.72 us  [the longest x1 0.99 us: local(): call(right_kernel, [((512, 256), BF16), ((8, 128), F32), ((16, 8, 8, 128)...]
  transfers between devices with their start and end apart: 3 -> 3, of which waited for: 2 -> 2; matrix products, arithmetic and copies ran while one was open for 0% -> 0% of each run, Pallas kernels for 0% -> 1%
where the time goes in v4:
time: 120 us
  blocking collectives  110 us (92%)
  Pallas kernels  6.53 us (5%)
    all_to_all x4, blocking collectives, exchange(): lax.all_to_all(x, ('row', 'col'), 0, 0, axis_index_groups=SAME_CORE, tile...  110 us
  transfers between devices with their start and end apart: 3, of which 2 were waited for; matrix products, arithmetic and copies ran while one was open for 0% of the time, Pallas kernels for 1%

profile of v4, /device:TPU:6, one launch (start us, length us, event | category | flops | bytes accessed | tf_op | source)
XLA Modules:
  0.0 119.6 jit_solution(10157425863775710648)
XLA Ops:
  0.6 1.1 pad_maximum_fusion.in_ref
  1.7 0.7 pack.1
  2.4 34.7 %all_to_all.20 = bf16[128,16,128]{2,1,0:T(8,128)(2,1)S(1)} all-to-all(bf16[128,16,128]{2,1,0:T(8,128)(2,1)S(1)} %pack.1), channel_id=1, replica_groups={{0,2,4,6,8,10,12,14,16,18,20,22,24,26,28,30,32,34,36,38,40,42,44,46,48,..., dimensions={0} | all-to-all | bytes 1048576 | tf_op jit(solution)/shard_map/all_to_all | solution.py:197
  37.1 0.4 left_order.1.a_ref
  37.5 0.1 collective-permute-start
  37.6 0.7 right_order.1
  38.4 0.8 collective-permute-done.other_ref
  39.2 0.5 pair.1
  39.7 0.0 copy-start
  39.7 0.0 copy-start.1
  39.7 0.0 copy-start.2
  39.7 26.4 %all_to_all.21 = f32[128,8,128]{2,1,0:T(8,128)S(1)} all-to-all(f32[128,8,128]{2,1,0:T(8,128)S(1)} %bitcast.21), channel_id=1, replica_groups={{0,2,4,6,8,10,12,14,16,18,20,22,24,26,28,30,32,34,36,38,40,42,44,46,48,..., dimensions={0} | all-to-all | bytes 1048576 | tf_op jit(solution)/shard_map/all_to_all | solution.py:197
  66.1 0.0 copy-done
  66.1 0.0 copy-done.1
  66.1 0.0 copy-done.2
  66.1 1.3 %norm.1 = (bf16[1024,128]{1,0:T(8,128)(2,1)}, bf16[1280,128]{1,0:T(8,128)(2,1)S(1)}) custom-call(f32[1024,128]{1,0:T(8,128)S(1)} %bitcast.20, bf16[1024,128]{1,0:T(8,128)(2,1)S(1)} %bitcast.25, bf16[1024,128]{1,0:T(8,128)(2,1)S(1)} %bitcast.26, bf16[128,128]{1,0:T(8,128)(2,1)S(1)} %copy-done.2), custom_call_target="tpu_custom_call" | custom-call | bytes 3000000 | tf_op jit(solution)/shard_map/norm/pallas_call | solution.py:227
  67.4 20.8 %all_to_all.22 = bf16[128,5,2,128]{3,2,1,0:T(2,128)(2,1)S(1)} all-to-all(bf16[128,5,2,128]{3,2,1,0:T(2,128)(2,1)S(1)} %bitcast.23), channel_id=1, replica_groups={{0,2,4,6,8,10,12,14,16,18,20,22,24,26,28,30,32,34,36,38,40,42,44,46,48,..., dimensions={0} | all-to-all | bytes 655360 | tf_op jit(solution)/shard_map/all_to_all | solution.py:197
  88.2 0.0 collective-permute-start.1
  88.2 0.5 collective-permute-start.2
  88.7 1.0 right.1
  89.7 0.3 collective-permute-done.2.got_ref
  90.0 0.0 collective-permute-done.1
  90.0 0.9 left.1
  90.9 27.7 %all_to_all.23 = bf16[128,9,2,128]{3,2,1,0:T(2,128)(2,1)S(1)} all-to-all(bf16[128,9,2,128]{3,2,1,0:T(2,128)(2,1)S(1)} %bitcast.18), channel_id=1, replica_groups={{0,2,4,6,8,10,12,14,16,18,20,22,24,26,28,30,32,34,36,38,40,42,44,46,48,..., dimensions={0} | all-to-all | bytes 1179648 | tf_op jit(solution)/shard_map/all_to_all | solution.py:197
  118.6 1.0 unpack.1
Async XLA Ops:
  37.5 1.6 %collective-permute-start = (bf16[512,256]{1,0:T(8,128)(2,1)S(1)}, bf16[512,256]{1,0:T(8,128)(2,1)S(1)}, u32[]{:S(2)}, u32[]{:S(2)}) collective-permute-start(bf16[512,256]{1,0:T(8,128)(2,1)S(1)} %left_order.1.a_ref), channel_id=1, source_target_pairs={{0,1},{1,0},{2,3},{3,2},{4,5},{5,4},{6,7},{7,6},{8,9},{9,8},{10,11... | collective-permute-start | bytes 786440 | tf_op jit(solution)/shard_map/ppermute | solution.py:201
  39.7 26.4 %copy-start = (bf16[32,32,128]{2,1,0:T(8,128)(2,1)S(1)}, bf16[32,32,128]{2,1,0:T(8,128)(2,1)}, u32[]{:S(2)}) copy-start(bf16[32,32,128]{2,1,0:T(8,128)(2,1)} %param.7) | copy-start | bytes 786436
  39.7 26.4 %copy-start.1 = (bf16[32,32,128]{2,1,0:T(8,128)(2,1)S(1)}, bf16[32,32,128]{2,1,0:T(8,128)(2,1)}, u32[]{:S(2)}) copy-start(bf16[32,32,128]{2,1,0:T(8,128)(2,1)} %param.9) | copy-start | bytes 786436
  39.7 26.4 %copy-start.2 = (bf16[128,128]{1,0:T(8,128)(2,1)S(1)}, bf16[128,128]{1,0:T(8,128)(2,1)}, u32[]{:S(2)}) copy-start(bf16[128,128]{1,0:T(8,128)(2,1)} %weight_ref.1) | copy-start | bytes 98308
  88.2 1.8 %collective-permute-start.1 = (bf16[128,5,2,128]{3,2,1,0:T(2,128)(2,1)S(1)}, bf16[128,5,2,128]{3,2,1,0:T(2,128)(2,1)S(1)}, u32[]{:S(2)}, u32[]{:S(2)}) collective-permute-start(bf16[128,5,2,128]{3,2,1,0:T(2,128)(2,1)S(1)} %all_to_all.22), channel_id=1, source_target_pairs={{0,1},{1,0},{2,3},{3,2},{4,5},{5,4},{6,7},{7,6},{8,9},{9,8},{10,11... | collective-permute-start | bytes 983048 | tf_op jit(solution)/shard_map/ppermute | solution.py:201
  88.2 1.8 %collective-permute-start.2 = (bf16[256,256]{1,0:T(8,128)(2,1)S(1)}, bf16[256,256]{1,0:T(8,128)(2,1)S(1)}, u32[]{:S(2)}, u32[]{:S(2)}) collective-permute-start(bf16[256,256]{1,0:T(8,128)(2,1)S(1)} %get-tuple-element.15.send_ref), channel_id=1, source_target_pairs={{0,1},{1,0},{2,3},{3,2},{4,5},{5,4},{6,7},{7,6},{8,9},{9,8},{10,11... | collective-permute-start | bytes 393224 | tf_op jit(solution)/shard_map/ppermute | solution.py:201

commit v5 on v4

--- a/solution.py
+++ b/solution.py
@@ -1,3 +1,5 @@
+import functools
+
 import jax
 import jax.numpy as jnp
 from jax import lax
@@ -10,6 +12,7 @@
 PARAMS = pltpu.CompilerParams(vmem_limit_bytes=32 * 1024 * 1024)
 NT = (((1,), (1,)), ((), ()))
 TN = (((0,), (0,)), ((), ()))
+FLOOR = 1e-07
 
 SAME_CORE = [[row * 16 + col for row in range(16) for col in range(core, 16, 2)] for core in (0, 1)]
 
@@ -79,7 +82,10 @@
             ref[:, pl.ds(g * 128, 128)] = nat[2 * which + g].astype(BF16)
 
 
-def pair_kernel(a_ref, other_ref, keep_ref, send_ref, out_ref, prod):
+def pair_kernel(a_ref, other_ref, keep_ref, send_ref, gate_ref, grad_ref, weight_ref, out_ref, gate_out, grad_out, weight_out, prod):
+    weight_out[...] = weight_ref[...]
+    gate_out[...] = gate_ref[...]
+    grad_out[...] = grad_ref[...]
     value = lax.dot_general(a_ref[...], keep_ref[...], NT, preferred_element_type=F32)
     value += lax.dot_general(other_ref[...], send_ref[...], NT, preferred_element_type=F32)
     for g in range(2):
@@ -91,7 +97,8 @@
                 out_ref[pl.ds(4 * rc, 4), 4 * g + t] = part.reshape(4, 8, 128)
 
 
-def norm_kernel(pair_ref, gate_ref, grad_ref, weight_ref, gate_out, out_ref, slabs):
+def norm_kernel(rounded, pair_ref, gate_ref, grad_ref, weight_ref, gate_out, out_ref, slabs):
+    worst = jnp.full((1, 128), -1.0, F32)
     weight = weight_ref[...]
     total = jnp.zeros((128, 128), F32)
     for s in range(8):
@@ -101,6 +108,7 @@
         centered = pair - average
         variance = jnp.mean(centered * centered, axis=0, keepdims=True)
         inv_std = lax.rsqrt(variance + 1e-05)
+        worst = jnp.maximum(worst, average * average + FLOOR - variance)
         normed = centered * inv_std
         normed_half = normed.astype(BF16)
         gate_prob = jax.nn.sigmoid(gate_ref[rows, :].astype(F32))
@@ -116,6 +124,8 @@
         grad_pair = (grad_normed - mean_one - normed * mean_two) * inv_std
         slabs[pl.ds(s, 128, stride=10), :] = grad_pair
     high, rest = split_halves(total * (1.0 / 512.0))
+    if rounded:
+        high = jnp.where(jnp.max(worst, axis=1, keepdims=True) > 0.0, jnp.inf, high)
     slabs[pl.ds(8, 128, stride=10), :] = high
     slabs[pl.ds(9, 128, stride=10), :] = rest
     out_ref[...] = slabs[...].astype(BF16)
@@ -156,8 +166,9 @@
                     out_ref[where] = part.reshape(4, 8, 128).astype(BF16)
 
 
-def left_kernel(far_ref, gp_ref, keep_ref, got_ref, sum_ref, right_ref, out_ref, raw, gp, prod, out):
+def left_kernel(far_ref, gp_ref, keep_ref, got_ref, sum_ref, right_ref, out_ref, flag_ref, raw, gp, prod, out):
     total = half_order(far_ref, raw, gp) + sum_ref[0:1, :]
+    flag_ref[0] = (jnp.max(total) > 3e38).astype(jnp.int32)
     high, rest = split_halves(total)
     out[pl.ds(16, 128, stride=18), :] = jnp.broadcast_to(high, (128, 128))
     out[pl.ds(17, 128, stride=18), :] = jnp.broadcast_to(rest, (128, 128))
@@ -185,7 +196,7 @@
         kernel,
         out_shape=[jax.ShapeDtypeStruct(s, d) for s, d in outs],
         in_specs=ins,
-        out_specs=[VM] * len(outs),
+        out_specs=[SM if s == (1,) else VM for s, _ in outs],
         scratch_shapes=[pltpu.VMEM(s, d) for s, d in scratch],
         compiler_params=PARAMS,
         cost_estimate=pl.CostEstimate(flops=0, bytes_accessed=3_000_000 * us, transcendentals=0),
@@ -220,43 +231,55 @@
         "right_order",
     )(core, blocks)
     got = other_core(send)
-    (pair,) = call(
-        pair_kernel, [((16, 8, 8, 128), F32)], [VM] * 4, [((2, 512, 128), F32)], "pair"
-    )(a, other, keep, send)
-    pair = exchange(pair.reshape(128, 8, 128))
-    grad_gate, grad_pair = call(
-        norm_kernel,
-        [((1024, 128), BF16), ((1280, 128), BF16)],
-        [VM] * 4,
-        [((1280, 128), F32)],
-        "norm",
-    )(pair.reshape(1024, 128), gate.reshape(1024, 128), grad_out.reshape(1024, 128), out_weight)
-    own = exchange(grad_pair.reshape(128, 5, 2, 128))
-    far = other_core(own)
-    half, total, right = call(
-        right_kernel,
-        [((512, 256), BF16), ((8, 128), F32), ((16, 8, 8, 128), BF16)],
-        [SM] + [VM] * 3,
-        [((1280, 128), F32), ((4, 256, 128), F32)],
-        "right",
-    )(core, own.reshape(1280, 128), a, other)
-    (grads,) = call(
-        left_kernel,
-        [((2304, 128), BF16)],
-        [VM] * 6,
-        [((1280, 128), F32), ((512, 256), BF16), ((2, 512, 128), F32), ((2304, 128), F32)],
-        "left",
-    )(far.reshape(1280, 128), half, keep, got, total, right)
-    grads = exchange(grads.reshape(128, 9, 2, 128))
-    grad_left, grad_right, grad_weight = call(
-        unpack_kernel,
-        [((1024, 128), BF16), ((1024, 128), BF16), ((128, 128), F32)],
-        [VM],
-        [((2304, 128), F32)],
-        "unpack",
-    )(grads.reshape(2304, 128))
+    other, got = lax.optimization_barrier((other, got))
+
+    def middle(dtype):
+        flat = (1024, 128)
+        pair, gates, ups, weight = call(
+            pair_kernel,
+            [((16, 8, 8, 128), F32), (flat, BF16), (flat, BF16), ((128, 128), BF16)],
+            [VM] * 7,
+            [((2, 512, 128), F32)],
+            "pair",
+        )(a, other, keep, send, gate.reshape(flat), grad_out.reshape(flat), out_weight)
+        pair = exchange(pair.reshape(128, 8, 128).astype(dtype)).astype(F32)
+        grad_gate, grad_pair = call(
+            functools.partial(norm_kernel, dtype != F32),
+            [((1024, 128), BF16), ((1280, 128), BF16)],
+            [VM] * 4,
+            [((1280, 128), F32)],
+            "norm",
+        )(pair.reshape(flat), gates, ups, weight)
+        own = exchange(grad_pair.reshape(128, 5, 2, 128))
+        far = other_core(own)
+        half, total, right = call(
+            right_kernel,
+            [((512, 256), BF16), ((8, 128), F32), ((16, 8, 8, 128), BF16)],
+            [SM] + [VM] * 3,
+            [((1280, 128), F32), ((4, 256, 128), F32)],
+            "right",
+        )(core, own.reshape(1280, 128), a, other)
+        grads, flag = call(
+            left_kernel,
+            [((2304, 128), BF16), ((1,), jnp.int32)],
+            [VM] * 6,
+            [((1280, 128), F32), ((512, 256), BF16), ((2, 512, 128), F32), ((2304, 128), F32)],
+            "left",
+        )(far.reshape(1280, 128), half, keep, got, total, right)
+        grads = exchange(grads.reshape(128, 9, 2, 128))
+        grad_left, grad_right, grad_weight = call(
+            unpack_kernel,
+            [((1024, 128), BF16), ((1024, 128), BF16), ((128, 128), F32)],
+            [VM],
+            [((2304, 128), F32)],
+            "unpack",
+        )(grads.reshape(2304, 128))
+        return flag[0], (grad_left, grad_right, grad_gate, grad_weight)
+
+    flag, outs = middle(jnp.float16)
+    left, right, gates, weight = lax.cond(flag > 0, lambda: middle(F32)[1], lambda: outs)
     shape = (32, 32, 128)
-    return grad_left.reshape(shape), grad_right.reshape(shape), grad_gate.reshape(shape), grad_weight
+    return left.reshape(shape), right.reshape(shape), gates.reshape(shape), weight
 
 
 def solution(mesh):

time: 120 us -> 117 us (0.975)
  blocking collectives: 110 us -> 76.7 us
  waiting for transfers between devices: 1.13 us -> 22.2 us
  starting transfers between devices: 0.6 us -> 7.52 us
    all_to_all x4 -> x3, blocking collectives: 110 us -> 76.7 us  [exchange(): lax.all_to_all(x, ('row', 'col'), 0, 0, axis_index_groups=SAME_CORE, tile...]
    all_to_all x0 -> x1, waiting for transfers between devices: none -> 20.6 us  [exchange(): lax.all_to_all(x, ('row', 'col'), 0, 0, axis_index_groups=SAME_CORE, tile...]
    all_to_all x0 -> x1, starting transfers between devices: none -> 6.84 us  [exchange(): lax.all_to_all(x, ('row', 'col'), 0, 0, axis_index_groups=SAME_CORE, tile...]
  transfers between devices with their start and end apart: 3 -> 4, of which waited for: 2 -> 3; matrix products, arithmetic and copies ran while one was open for 0% -> 0% of each run, Pallas kernels for 1% -> 1%
where the time goes in v5:
time: 117 us; the launch traced here: 116 us
  blocking collectives  76.7 us (66%)
  waiting for transfers between devices  22.2 us (19%)
  starting transfers between devices  7.52 us (6%)
  Pallas kernels  7.45 us (6%)
  between operations  1.39 us (1%)
    all_to_all x3, blocking collectives, exchange(): lax.all_to_all(x, ('row', 'col'), 0, 0, axis_index_groups=SAME_CORE, tile...  76.7 us
    all_to_all x1, waiting for transfers between devices, exchange(): lax.all_to_all(x, ('row', 'col'), 0, 0, axis_index_groups=SAME_CORE, tile...  20.6 us
    all_to_all x1, starting transfers between devices, exchange(): lax.all_to_all(x, ('row', 'col'), 0, 0, axis_index_groups=SAME_CORE, tile...  6.84 us
  transfers between devices with their start and end apart: 4, of which 3 were waited for; matrix products, arithmetic and copies ran while one was open for 0% of the time, Pallas kernels for 1%

profile of v5, /device:TPU:6, one launch (start us, length us, event | category | flops | bytes accessed | tf_op | source)
XLA Modules:
  0.0 116.4 jit_solution(696368374084499209)
XLA Ops:
  0.6 1.1 pad_maximum_fusion.in_ref
  1.7 0.7 pack.1
  2.4 34.7 %all_to_all.35 = bf16[128,16,128]{2,1,0:T(8,128)(2,1)S(1)} all-to-all(bf16[128,16,128]{2,1,0:T(8,128)(2,1)S(1)} %pack.1), channel_id=1, replica_groups={{0,2,4,6,8,10,12,14,16,18,20,22,24,26,28,30,32,34,36,38,40,42,44,46,48,..., dimensions={0} | all-to-all | bytes 1048576 | tf_op jit(solution)/shard_map/all_to_all | solution.py:208
  37.1 0.0 copy-start.2
  37.1 0.4 left_order.1.a_ref
  37.5 0.0 copy-start
  37.6 0.0 copy-start.1
  37.6 0.1 collective-permute-start.1
  37.7 0.7 right_order.1
  38.4 0.6 collective-permute-start.2
  39.0 1.0 collective-permute-done.2.got_ref
  39.9 0.0 collective-permute-done.1.other_ref
  39.9 0.0 copy-done.2
  40.0 0.0 copy-done
  40.0 0.0 copy-done.1
  40.0 0.6 pair.3
  40.6 20.9 %all_to_all.36 = f16[128,8,128]{2,1,0:T(8,128)(2,1)S(1)} all-to-all(f16[128,8,128]{2,1,0:T(8,128)(2,1)S(1)} %bitcast.41), channel_id=1, replica_groups={{0,2,4,6,8,10,12,14,16,18,20,22,24,26,28,30,32,34,36,38,40,42,44,46,48,..., dimensions={0} | all-to-all | bytes 524288 | tf_op jit(solution)/shard_map/all_to_all | solution.py:208
  61.5 1.3 %norm.3 = (bf16[1024,128]{1,0:T(8,128)(2,1)}, bf16[1280,128]{1,0:T(8,128)(2,1)S(1)}) custom-call(f32[1024,128]{1,0:T(8,128)S(1)} %bitcast_convert_fusion.pair_ref, bf16[1024,128]{1,0:T(8,128)(2,1)S(1)} %get-tuple-element.89.gate_ref, bf16[1024,128]{1,0:T(8,128)(2,1)S(1)} %get-tuple-element.90.grad_ref, bf16[128,128]{1,0:T(8,128)(2,1)S(1)} %get-tuple-element.91.weight_ref), custom_call_target="tpu_custom_call" | custom-call | bytes 3000000 | tf_op jit(solution)/shard_map/norm/pallas_call | solution.py:246
  62.8 21.1 %all_to_all.37 = bf16[128,5,2,128]{3,2,1,0:T(2,128)(2,1)S(1)} all-to-all(bf16[128,5,2,128]{3,2,1,0:T(2,128)(2,1)S(1)} %bitcast.38), channel_id=1, replica_groups={{0,2,4,6,8,10,12,14,16,18,20,22,24,26,28,30,32,34,36,38,40,42,44,46,48,..., dimensions={0} | all-to-all | bytes 655360 | tf_op jit(solution)/shard_map/all_to_all | solution.py:208
  84.0 0.0 collective-permute-start.3
  84.0 1.0 right.3
  85.0 0.6 collective-permute-done.3
  85.6 1.7 %left.3 = (bf16[2304,128]{1,0:T(8,128)(2,1)}, s32[1]{0:T(128)}) custom-call(bf16[1280,128]{1,0:T(8,128)(2,1)S(1)} %bitcast.39, bf16[512,256]{1,0:T(8,128)(2,1)S(1)} %get-tuple-element.93.gp_ref, bf16[256,256]{1,0:T(8,128)(2,1)S(1)} %get-tuple-element.87.keep_ref, bf16[256,256]{1,0:T(8,128)(2,1)S(1)} %collective-permute-done.2.got_ref, ...), custom_call_target="tpu_custom_call" | custom-call | bytes 3000000 | tf_op jit(solution)/shard_map/left/pallas_call | solution.py:262
  87.3 6.8 %all-to-all-start.6 = ((bf16[128,9,2,128]{3,2,1,0:T(2,128)(2,1)}), bf16[128,9,2,128]{3,2,1,0:T(2,128)(2,1)S(1)}, u32[]{:S(2)}, u32[]{:S(2)}) async-start(bf16[128,9,2,128]{3,2,1,0:T(2,128)(2,1)} %bitcast.21), calls=%async_computation.6 | async-start | bytes 1179648 | tf_op jit(solution)/shard_map/all_to_all | solution.py:208
  94.8 20.6 %all-to-all-done.6 = bf16[128,9,2,128]{3,2,1,0:T(2,128)(2,1)S(1)} async-done(((bf16[128,9,2,128]{3,2,1,0:T(2,128)(2,1)}), bf16[128,9,2,128]{3,2,1,0:T(2,128)(2,1)S(1)}, u32[]{:S(2)}, u32[]{:S(2)}) %all-to-all-start.6) | async-done | bytes 589856 | tf_op jit(solution)/shard_map/all_to_all | solution.py:208
  115.4 1.0 unpack.3
  (3 shorter events, 0.1 us)
Async XLA Ops:
  37.1 2.8 %copy-start.2 = (bf16[128,128]{1,0:T(8,128)(2,1)S(1)}, bf16[128,128]{1,0:T(8,128)(2,1)}, u32[]{:S(2)}) copy-start(bf16[128,128]{1,0:T(8,128)(2,1)} %weight_ref.1) | copy-start | bytes 98308
  37.5 2.4 %copy-start = (bf16[32,32,128]{2,1,0:T(8,128)(2,1)S(1)}, bf16[32,32,128]{2,1,0:T(8,128)(2,1)}, u32[]{:S(2)}) copy-start(bf16[32,32,128]{2,1,0:T(8,128)(2,1)} %param.9) | copy-start | bytes 786436
  37.6 2.4 %copy-start.1 = (bf16[32,32,128]{2,1,0:T(8,128)(2,1)S(1)}, bf16[32,32,128]{2,1,0:T(8,128)(2,1)}, u32[]{:S(2)}) copy-start(bf16[32,32,128]{2,1,0:T(8,128)(2,1)} %param.11) | copy-start | bytes 786436
  37.6 2.4 %collective-permute-start.1 = (bf16[512,256]{1,0:T(8,128)(2,1)S(1)}, bf16[512,256]{1,0:T(8,128)(2,1)S(1)}, u32[]{:S(2)}, u32[]{:S(2)}) collective-permute-start(bf16[512,256]{1,0:T(8,128)(2,1)S(1)} %left_order.1.a_ref), channel_id=1, source_target_pairs={{0,1},{1,0},{2,3},{3,2},{4,5},{5,4},{6,7},{7,6},{8,9},{9,8},{10,11... | collective-permute-start | bytes 786440 | tf_op jit(solution)/shard_map/ppermute | solution.py:212
  38.4 1.6 %collective-permute-start.2 = (bf16[256,256]{1,0:T(8,128)(2,1)S(1)}, bf16[256,256]{1,0:T(8,128)(2,1)S(1)}, u32[]{:S(2)}, u32[]{:S(2)}) collective-permute-start(bf16[256,256]{1,0:T(8,128)(2,1)S(1)} %get-tuple-element.85.send_ref), channel_id=1, source_target_pairs={{0,1},{1,0},{2,3},{3,2},{4,5},{5,4},{6,7},{7,6},{8,9},{9,8},{10,11... | collective-permute-start | bytes 393224 | tf_op jit(solution)/shard_map/ppermute | solution.py:212
  84.0 1.6 %collective-permute-start.3 = (bf16[128,5,2,128]{3,2,1,0:T(2,128)(2,1)S(1)}, bf16[128,5,2,128]{3,2,1,0:T(2,128)(2,1)S(1)}, u32[]{:S(2)}, u32[]{:S(2)}) collective-permute-start(bf16[128,5,2,128]{3,2,1,0:T(2,128)(2,1)S(1)} %all_to_all.37), channel_id=1, source_target_pairs={{0,1},{1,0},{2,3},{3,2},{4,5},{5,4},{6,7},{7,6},{8,9},{9,8},{10,11... | collective-permute-start | bytes 983048 | tf_op jit(solution)/shard_map/ppermute | solution.py:212
  87.3 28.1 %all-to-all-start.6 = ((bf16[128,9,2,128]{3,2,1,0:T(2,128)(2,1)}), bf16[128,9,2,128]{3,2,1,0:T(2,128)(2,1)S(1)}, u32[]{:S(2)}, u32[]{:S(2)}) async-start(bf16[128,9,2,128]{3,2,1,0:T(2,128)(2,1)} %bitcast.21), calls=%async_computation.6 | async-start | bytes 1179648 | tf_op jit(solution)/shard_map/all_to_all | solution.py:208

commit v6 on v5

--- a/solution.py
+++ b/solution.py
@@ -230,8 +230,6 @@
         [((16, 8, 8, 128), F32), ((4, 256, 128), F32)],
         "right_order",
     )(core, blocks)
-    got = other_core(send)
-    other, got = lax.optimization_barrier((other, got))
 
     def middle(dtype):
         flat = (1024, 128)
@@ -252,6 +250,7 @@
         )(pair.reshape(flat), gates, ups, weight)
         own = exchange(grad_pair.reshape(128, 5, 2, 128))
         far = other_core(own)
+        got = other_core(send)
         half, total, right = call(
             right_kernel,
             [((512, 256), BF16), ((8, 128), F32), ((16, 8, 8, 128), BF16)],

time: 117 us -> 116 us (level)
  no operation moved by 1% of the time
where the time goes in v6:
time: 116 us; the launch traced here: 115 us
  blocking collectives  76.3 us (66%)
  waiting for transfers between devices  21.7 us (19%)
  Pallas kernels  7.47 us (6%)
  starting transfers between devices  7.44 us (6%)
  between operations  1.39 us (1%)
    all_to_all x3, blocking collectives, exchange(): lax.all_to_all(x, ('row', 'col'), 0, 0, axis_index_groups=SAME_CORE, tile...  76.3 us
    all_to_all x1, waiting for transfers between devices, exchange(): lax.all_to_all(x, ('row', 'col'), 0, 0, axis_index_groups=SAME_CORE, tile...  20.6 us
    all_to_all x1, starting transfers between devices, exchange(): lax.all_to_all(x, ('row', 'col'), 0, 0, axis_index_groups=SAME_CORE, tile...  6.84 us
  transfers between devices with their start and end apart: 4, of which 3 were waited for; matrix products, arithmetic and copies ran while one was open for 0% of the time, Pallas kernels for 1%

profile of v6, /device:TPU:6, one launch (start us, length us, event | category | flops | bytes accessed | tf_op | source)
XLA Modules:
  0.0 115.4 jit_solution(11808421539712026085)
XLA Ops:
  0.6 1.1 pad_maximum_fusion.in_ref
  1.7 0.7 pack.1
  2.4 34.7 %all_to_all.35 = bf16[128,16,128]{2,1,0:T(8,128)(2,1)S(1)} all-to-all(bf16[128,16,128]{2,1,0:T(8,128)(2,1)S(1)} %pack.1), channel_id=1, replica_groups={{0,2,4,6,8,10,12,14,16,18,20,22,24,26,28,30,32,34,36,38,40,42,44,46,48,..., dimensions={0} | all-to-all | bytes 1048576 | tf_op jit(solution)/shard_map/all_to_all | solution.py:208
  37.1 0.0 copy-start.2
  37.1 0.4 left_order.1.a_ref
  37.5 0.0 copy-start
  37.6 0.0 copy-start.1
  37.6 0.1 collective-permute-start.2
  37.7 0.7 right_order.1
  38.4 0.8 collective-permute-done.2.other_ref
  39.2 0.0 copy-done.2
  39.2 0.0 copy-done
  39.2 0.0 copy-done.1
  39.2 0.6 pair.3
  39.8 20.7 %all_to_all.36 = f16[128,8,128]{2,1,0:T(8,128)(2,1)S(1)} all-to-all(f16[128,8,128]{2,1,0:T(8,128)(2,1)S(1)} %bitcast.41), channel_id=1, replica_groups={{0,2,4,6,8,10,12,14,16,18,20,22,24,26,28,30,32,34,36,38,40,42,44,46,48,..., dimensions={0} | all-to-all | bytes 524288 | tf_op jit(solution)/shard_map/all_to_all | solution.py:208
  60.6 1.3 %norm.3 = (bf16[1024,128]{1,0:T(8,128)(2,1)}, bf16[1280,128]{1,0:T(8,128)(2,1)S(1)}) custom-call(f32[1024,128]{1,0:T(8,128)S(1)} %bitcast_convert_fusion.pair_ref, bf16[1024,128]{1,0:T(8,128)(2,1)S(1)} %get-tuple-element.83.gate_ref, bf16[1024,128]{1,0:T(8,128)(2,1)S(1)} %get-tuple-element.84.grad_ref, bf16[128,128]{1,0:T(8,128)(2,1)S(1)} %get-tuple-element.85.weight_ref), custom_call_target="tpu_custom_call" | custom-call | bytes 3000000 | tf_op jit(solution)/shard_map/norm/pallas_call | solution.py:244
  61.9 20.9 %all_to_all.37 = bf16[128,5,2,128]{3,2,1,0:T(2,128)(2,1)S(1)} all-to-all(bf16[128,5,2,128]{3,2,1,0:T(2,128)(2,1)S(1)} %bitcast.38), channel_id=1, replica_groups={{0,2,4,6,8,10,12,14,16,18,20,22,24,26,28,30,32,34,36,38,40,42,44,46,48,..., dimensions={0} | all-to-all | bytes 655360 | tf_op jit(solution)/shard_map/all_to_all | solution.py:208
  82.8 0.0 collective-permute-start.3
  82.8 0.5 collective-permute-start.4
  83.3 1.0 right.3
  84.3 0.3 collective-permute-done.4.got_ref
  84.6 0.0 collective-permute-done.3
  84.6 1.7 %left.3 = (bf16[2304,128]{1,0:T(8,128)(2,1)}, s32[1]{0:T(128)}) custom-call(bf16[1280,128]{1,0:T(8,128)(2,1)S(1)} %bitcast.39, bf16[512,256]{1,0:T(8,128)(2,1)S(1)} %get-tuple-element.87.gp_ref, bf16[256,256]{1,0:T(8,128)(2,1)S(1)} %get-tuple-element.80.keep_ref, bf16[256,256]{1,0:T(8,128)(2,1)S(1)} %collective-permute-done.4.got_ref, ...), custom_call_target="tpu_custom_call" | custom-call | bytes 3000000 | tf_op jit(solution)/shard_map/left/pallas_call | solution.py:261
  86.4 6.8 %all-to-all-start.6 = ((bf16[128,9,2,128]{3,2,1,0:T(2,128)(2,1)}), bf16[128,9,2,128]{3,2,1,0:T(2,128)(2,1)S(1)}, u32[]{:S(2)}, u32[]{:S(2)}) async-start(bf16[128,9,2,128]{3,2,1,0:T(2,128)(2,1)} %bitcast.21), calls=%async_computation.6 | async-start | bytes 1179648 | tf_op jit(solution)/shard_map/all_to_all | solution.py:208
  93.9 20.6 %all-to-all-done.6 = bf16[128,9,2,128]{3,2,1,0:T(2,128)(2,1)S(1)} async-done(((bf16[128,9,2,128]{3,2,1,0:T(2,128)(2,1)}), bf16[128,9,2,128]{3,2,1,0:T(2,128)(2,1)S(1)}, u32[]{:S(2)}, u32[]{:S(2)}) %all-to-all-start.6) | async-done | bytes 589856 | tf_op jit(solution)/shard_map/all_to_all | solution.py:208
  114.4 1.0 unpack.3
  (3 shorter events, 0.1 us)
Async XLA Ops:
  37.1 2.1 %copy-start.2 = (bf16[128,128]{1,0:T(8,128)(2,1)S(1)}, bf16[128,128]{1,0:T(8,128)(2,1)}, u32[]{:S(2)}) copy-start(bf16[128,128]{1,0:T(8,128)(2,1)} %weight_ref.1) | copy-start | bytes 98308
  37.5 1.7 %copy-start = (bf16[32,32,128]{2,1,0:T(8,128)(2,1)S(1)}, bf16[32,32,128]{2,1,0:T(8,128)(2,1)}, u32[]{:S(2)}) copy-start(bf16[32,32,128]{2,1,0:T(8,128)(2,1)} %param.9) | copy-start | bytes 786436
  37.6 1.6 %copy-start.1 = (bf16[32,32,128]{2,1,0:T(8,128)(2,1)S(1)}, bf16[32,32,128]{2,1,0:T(8,128)(2,1)}, u32[]{:S(2)}) copy-start(bf16[32,32,128]{2,1,0:T(8,128)(2,1)} %param.11) | copy-start | bytes 786436
  37.6 1.6 %collective-permute-start.2 = (bf16[512,256]{1,0:T(8,128)(2,1)S(1)}, bf16[512,256]{1,0:T(8,128)(2,1)S(1)}, u32[]{:S(2)}, u32[]{:S(2)}) collective-permute-start(bf16[512,256]{1,0:T(8,128)(2,1)S(1)} %left_order.1.a_ref), channel_id=1, source_target_pairs={{0,1},{1,0},{2,3},{3,2},{4,5},{5,4},{6,7},{7,6},{8,9},{9,8},{10,11... | collective-permute-start | bytes 786440 | tf_op jit(solution)/shard_map/ppermute | solution.py:212
  82.8 1.8 %collective-permute-start.3 = (bf16[128,5,2,128]{3,2,1,0:T(2,128)(2,1)S(1)}, bf16[128,5,2,128]{3,2,1,0:T(2,128)(2,1)S(1)}, u32[]{:S(2)}, u32[]{:S(2)}) collective-permute-start(bf16[128,5,2,128]{3,2,1,0:T(2,128)(2,1)S(1)} %all_to_all.37), channel_id=1, source_target_pairs={{0,1},{1,0},{2,3},{3,2},{4,5},{5,4},{6,7},{7,6},{8,9},{9,8},{10,11... | collective-permute-start | bytes 983048 | tf_op jit(solution)/shard_map/ppermute | solution.py:212
  82.8 1.8 %collective-permute-start.4 = (bf16[256,256]{1,0:T(8,128)(2,1)S(1)}, bf16[256,256]{1,0:T(8,128)(2,1)S(1)}, u32[]{:S(2)}, u32[]{:S(2)}) collective-permute-start(bf16[256,256]{1,0:T(8,128)(2,1)S(1)} %get-tuple-element.81.send_ref), channel_id=1, source_target_pairs={{0,1},{1,0},{2,3},{3,2},{4,5},{5,4},{6,7},{7,6},{8,9},{9,8},{10,11... | collective-permute-start | bytes 393224 | tf_op jit(solution)/shard_map/ppermute | solution.py:212
  86.4 28.0 %all-to-all-start.6 = ((bf16[128,9,2,128]{3,2,1,0:T(2,128)(2,1)}), bf16[128,9,2,128]{3,2,1,0:T(2,128)(2,1)S(1)}, u32[]{:S(2)}, u32[]{:S(2)}) async-start(bf16[128,9,2,128]{3,2,1,0:T(2,128)(2,1)} %bitcast.21), calls=%async_computation.6 | async-start | bytes 1179648 | tf_op jit(solution)/shard_map/all_to_all | solution.py:208

commit v7 on v6

--- a/solution.py
+++ b/solution.py
@@ -147,7 +147,7 @@
     return jnp.sum(terms[0], axis=0, keepdims=True) + jnp.sum(terms[1], axis=0, keepdims=True)
 
 
-def right_kernel(core_ref, own_ref, a_ref, other_ref, gp_ref, sum_ref, out_ref, raw, flat):
+def right_kernel(core_ref, own_ref, a_ref, other_ref, gate_ref, gp_ref, sum_ref, out_ref, raw, flat):
     core = core_ref[0]
     sum_ref[...] = jnp.broadcast_to(half_order(own_ref, raw, gp_ref), (8, 128))
     turned = gp_ref[...].T
@@ -254,10 +254,10 @@
         half, total, right = call(
             right_kernel,
             [((512, 256), BF16), ((8, 128), F32), ((16, 8, 8, 128), BF16)],
-            [SM] + [VM] * 3,
+            [SM] + [VM] * 4,
             [((1280, 128), F32), ((4, 256, 128), F32)],
             "right",
-        )(core, own.reshape(1280, 128), a, other)
+        )(core, own.reshape(1280, 128), a, other, grad_gate)
         grads, flag = call(
             left_kernel,
             [((2304, 128), BF16), ((1,), jnp.int32)],

time: 116 us -> 115 us (level)
  no operation moved by 1% of the time
where the time goes in v7:
time: 115 us
  blocking collectives  76.3 us (66%)
  waiting for transfers between devices  21.7 us (19%)
  starting transfers between devices  7.44 us (6%)
  Pallas kernels  6.82 us (6%)
  between operations  1.41 us (1%)
    all_to_all x3, blocking collectives, exchange(): lax.all_to_all(x, ('row', 'col'), 0, 0, axis_index_groups=SAME_CORE, tile...  76.3 us
    all_to_all x1, waiting for transfers between devices, exchange(): lax.all_to_all(x, ('row', 'col'), 0, 0, axis_index_groups=SAME_CORE, tile...  20.6 us
    all_to_all x1, starting transfers between devices, exchange(): lax.all_to_all(x, ('row', 'col'), 0, 0, axis_index_groups=SAME_CORE, tile...  6.84 us
  transfers between devices with their start and end apart: 4, of which 3 were waited for; matrix products, arithmetic and copies ran while one was open for 0% of the time, Pallas kernels for 1%

profile of v7, /device:TPU:6, one launch (start us, length us, event | category | flops | bytes accessed | tf_op | source)
XLA Modules:
  0.0 114.8 jit_solution(13736402452274465230)
XLA Ops:
  0.6 1.1 pad_maximum_fusion.in_ref
  1.7 0.7 pack.1
  2.4 34.7 %all_to_all.35 = bf16[128,16,128]{2,1,0:T(8,128)(2,1)S(1)} all-to-all(bf16[128,16,128]{2,1,0:T(8,128)(2,1)S(1)} %pack.1), channel_id=1, replica_groups={{0,2,4,6,8,10,12,14,16,18,20,22,24,26,28,30,32,34,36,38,40,42,44,46,48,..., dimensions={0} | all-to-all | bytes 1048576 | tf_op jit(solution)/shard_map/all_to_all | solution.py:208
  37.1 0.0 copy-start.4
  37.1 0.4 left_order.1.a_ref
  37.5 0.0 copy-start
  37.6 0.0 copy-start.1
  37.6 0.1 collective-permute-start.2
  37.7 0.7 right_order.1
  38.4 0.8 collective-permute-done.2.other_ref
  39.2 0.0 copy-done.4
  39.2 0.0 copy-done
  39.2 0.0 copy-done.1
  39.2 0.6 pair.3
  39.8 20.7 %all_to_all.36 = f16[128,8,128]{2,1,0:T(8,128)(2,1)S(1)} all-to-all(f16[128,8,128]{2,1,0:T(8,128)(2,1)S(1)} %bitcast.41), channel_id=1, replica_groups={{0,2,4,6,8,10,12,14,16,18,20,22,24,26,28,30,32,34,36,38,40,42,44,46,48,..., dimensions={0} | all-to-all | bytes 524288 | tf_op jit(solution)/shard_map/all_to_all | solution.py:208
  60.6 0.6 norm.3
  61.2 0.0 copy-start.2
  61.2 20.9 %all_to_all.37 = bf16[128,5,2,128]{3,2,1,0:T(2,128)(2,1)S(1)} all-to-all(bf16[128,5,2,128]{3,2,1,0:T(2,128)(2,1)S(1)} %bitcast.38), channel_id=1, replica_groups={{0,2,4,6,8,10,12,14,16,18,20,22,24,26,28,30,32,34,36,38,40,42,44,46,48,..., dimensions={0} | all-to-all | bytes 655360 | tf_op jit(solution)/shard_map/all_to_all | solution.py:208
  82.2 0.0 collective-permute-start.3
  82.2 0.5 collective-permute-start.4
  82.7 1.0 right.3
  83.7 0.0 copy-done.2
  83.7 0.3 collective-permute-done.4.got_ref
  84.0 0.0 collective-permute-done.3
  84.0 1.8 %left.3 = (bf16[2304,128]{1,0:T(8,128)(2,1)}, s32[1]{0:T(128)}) custom-call(bf16[1280,128]{1,0:T(8,128)(2,1)S(1)} %bitcast.39, bf16[512,256]{1,0:T(8,128)(2,1)S(1)} %get-tuple-element.88.gp_ref, bf16[256,256]{1,0:T(8,128)(2,1)S(1)} %get-tuple-element.80.keep_ref, bf16[256,256]{1,0:T(8,128)(2,1)S(1)} %collective-permute-done.4.got_ref, ...), custom_call_target="tpu_custom_call" | custom-call | bytes 3000000 | tf_op jit(solution)/shard_map/left/pallas_call | solution.py:261
  85.7 6.8 %all-to-all-start.6 = ((bf16[128,9,2,128]{3,2,1,0:T(2,128)(2,1)}), bf16[128,9,2,128]{3,2,1,0:T(2,128)(2,1)S(1)}, u32[]{:S(2)}, u32[]{:S(2)}) async-start(bf16[128,9,2,128]{3,2,1,0:T(2,128)(2,1)} %bitcast.21), calls=%async_computation.6 | async-start | bytes 1179648 | tf_op jit(solution)/shard_map/all_to_all | solution.py:208
  93.2 20.6 %all-to-all-done.6 = bf16[128,9,2,128]{3,2,1,0:T(2,128)(2,1)S(1)} async-done(((bf16[128,9,2,128]{3,2,1,0:T(2,128)(2,1)}), bf16[128,9,2,128]{3,2,1,0:T(2,128)(2,1)S(1)}, u32[]{:S(2)}, u32[]{:S(2)}) %all-to-all-start.6) | async-done | bytes 589856 | tf_op jit(solution)/shard_map/all_to_all | solution.py:208
  113.8 1.0 unpack.3
  (3 shorter events, 0.1 us)
Async XLA Ops:
  37.1 2.1 %copy-start.4 = (bf16[128,128]{1,0:T(8,128)(2,1)S(1)}, bf16[128,128]{1,0:T(8,128)(2,1)}, u32[]{:S(2)}) copy-start(bf16[128,128]{1,0:T(8,128)(2,1)} %weight_ref.1) | copy-start | bytes 98308
  37.5 1.7 %copy-start = (bf16[32,32,128]{2,1,0:T(8,128)(2,1)S(1)}, bf16[32,32,128]{2,1,0:T(8,128)(2,1)}, u32[]{:S(2)}) copy-start(bf16[32,32,128]{2,1,0:T(8,128)(2,1)} %param.9) | copy-start | bytes 786436
  37.6 1.6 %copy-start.1 = (bf16[32,32,128]{2,1,0:T(8,128)(2,1)S(1)}, bf16[32,32,128]{2,1,0:T(8,128)(2,1)}, u32[]{:S(2)}) copy-start(bf16[32,32,128]{2,1,0:T(8,128)(2,1)} %param.11) | copy-start | bytes 786436
  37.6 1.6 %collective-permute-start.2 = (bf16[512,256]{1,0:T(8,128)(2,1)S(1)}, bf16[512,256]{1,0:T(8,128)(2,1)S(1)}, u32[]{:S(2)}, u32[]{:S(2)}) collective-permute-start(bf16[512,256]{1,0:T(8,128)(2,1)S(1)} %left_order.1.a_ref), channel_id=1, source_target_pairs={{0,1},{1,0},{2,3},{3,2},{4,5},{5,4},{6,7},{7,6},{8,9},{9,8},{10,11... | collective-permute-start | bytes 786440 | tf_op jit(solution)/shard_map/ppermute | solution.py:212
  61.2 22.5 %copy-start.2 = (bf16[1024,128]{1,0:T(8,128)(2,1)}, bf16[1024,128]{1,0:T(8,128)(2,1)S(1)}, u32[]{:S(2)}) copy-start(bf16[1024,128]{1,0:T(8,128)(2,1)S(1)} %get-tuple-element.87.gate_ref) | copy-start | bytes 786436
  82.2 1.8 %collective-permute-start.3 = (bf16[128,5,2,128]{3,2,1,0:T(2,128)(2,1)S(1)}, bf16[128,5,2,128]{3,2,1,0:T(2,128)(2,1)S(1)}, u32[]{:S(2)}, u32[]{:S(2)}) collective-permute-start(bf16[128,5,2,128]{3,2,1,0:T(2,128)(2,1)S(1)} %all_to_all.37), channel_id=1, source_target_pairs={{0,1},{1,0},{2,3},{3,2},{4,5},{5,4},{6,7},{7,6},{8,9},{9,8},{10,11... | collective-permute-start | bytes 983048 | tf_op jit(solution)/shard_map/ppermute | solution.py:212
  82.2 1.8 %collective-permute-start.4 = (bf16[256,256]{1,0:T(8,128)(2,1)S(1)}, bf16[256,256]{1,0:T(8,128)(2,1)S(1)}, u32[]{:S(2)}, u32[]{:S(2)}) collective-permute-start(bf16[256,256]{1,0:T(8,128)(2,1)S(1)} %get-tuple-element.81.send_ref), channel_id=1, source_target_pairs={{0,1},{1,0},{2,3},{3,2},{4,5},{5,4},{6,7},{7,6},{8,9},{9,8},{10,11... | collective-permute-start | bytes 393224 | tf_op jit(solution)/shard_map/ppermute | solution.py:212
  85.7 28.1 %all-to-all-start.6 = ((bf16[128,9,2,128]{3,2,1,0:T(2,128)(2,1)}), bf16[128,9,2,128]{3,2,1,0:T(2,128)(2,1)S(1)}, u32[]{:S(2)}, u32[]{:S(2)}) async-start(bf16[128,9,2,128]{3,2,1,0:T(2,128)(2,1)} %bitcast.21), calls=%async_computation.6 | async-start | bytes 1179648 | tf_op jit(solution)/shard_map/all_to_all | solution.py:208

commit v8 on v7

--- a/solution.py
+++ b/solution.py
@@ -240,6 +240,8 @@
             [((2, 512, 128), F32)],
             "pair",
         )(a, other, keep, send, gate.reshape(flat), grad_out.reshape(flat), out_weight)
+        got = other_core(send)
+        pair, got = lax.optimization_barrier((pair, got))
         pair = exchange(pair.reshape(128, 8, 128).astype(dtype)).astype(F32)
         grad_gate, grad_pair = call(
             functools.partial(norm_kernel, dtype != F32),
@@ -250,7 +252,6 @@
         )(pair.reshape(flat), gates, ups, weight)
         own = exchange(grad_pair.reshape(128, 5, 2, 128))
         far = other_core(own)
-        got = other_core(send)
         half, total, right = call(
             right_kernel,
             [((512, 256), BF16), ((8, 128), F32), ((16, 8, 8, 128), BF16)],

time: 115 us -> 116 us (level)
  transfers between devices with their start and end apart: 4 -> 4, of which waited for: 3 -> 4; matrix products, arithmetic and copies ran while one was open for 0% -> 0% of each run, Pallas kernels for 1% -> 2%
where the time goes in v8:
time: 116 us; the launch traced here: 115 us
  blocking collectives  76.7 us (66%)
  waiting for transfers between devices  21.6 us (19%)
  starting transfers between devices  7.52 us (6%)
  Pallas kernels  6.81 us (6%)
  between operations  1.41 us (1%)
    all_to_all x3, blocking collectives, exchange(): lax.all_to_all(x, ('row', 'col'), 0, 0, axis_index_groups=SAME_CORE, tile...  76.7 us
    all_to_all x1, waiting for transfers between devices, exchange(): lax.all_to_all(x, ('row', 'col'), 0, 0, axis_index_groups=SAME_CORE, tile...  20.6 us
    all_to_all x1, starting transfers between devices, exchange(): lax.all_to_all(x, ('row', 'col'), 0, 0, axis_index_groups=SAME_CORE, tile...  6.84 us
  transfers between devices with their start and end apart: 4, of which 4 were waited for; matrix products, arithmetic and copies ran while one was open for 0% of the time, Pallas kernels for 2%

profile of v8, /device:TPU:6, one launch (start us, length us, event | category | flops | bytes accessed | tf_op | source)
XLA Modules:
  0.0 115.2 jit_solution(853464408163616673)
XLA Ops:
  0.6 1.1 pad_maximum_fusion.in_ref
  1.7 0.7 pack.1
  2.4 34.7 %all_to_all.35 = bf16[128,16,128]{2,1,0:T(8,128)(2,1)S(1)} all-to-all(bf16[128,16,128]{2,1,0:T(8,128)(2,1)S(1)} %pack.1), channel_id=1, replica_groups={{0,2,4,6,8,10,12,14,16,18,20,22,24,26,28,30,32,34,36,38,40,42,44,46,48,..., dimensions={0} | all-to-all | bytes 1048576 | tf_op jit(solution)/shard_map/all_to_all | solution.py:208
  37.1 0.0 copy-start.4
  37.1 0.4 left_order.1.a_ref
  37.5 0.0 copy-start
  37.6 0.0 copy-start.1
  37.6 0.1 collective-permute-start.2
  37.7 0.7 right_order.1
  38.4 0.6 collective-permute-start.3
  39.0 0.2 collective-permute-done.2.other_ref
  39.2 0.0 copy-done.4
  39.2 0.0 copy-done
  39.2 0.0 copy-done.1
  39.2 0.6 pair.3
  39.8 0.2 collective-permute-done.3.got_ref
  40.0 20.9 %all_to_all.36 = f16[128,8,128]{2,1,0:T(8,128)(2,1)S(1)} all-to-all(f16[128,8,128]{2,1,0:T(8,128)(2,1)S(1)} %bitcast.41), channel_id=1, replica_groups={{0,2,4,6,8,10,12,14,16,18,20,22,24,26,28,30,32,34,36,38,40,42,44,46,48,..., dimensions={0} | all-to-all | bytes 524288 | tf_op jit(solution)/shard_map/all_to_all | solution.py:208
  60.9 0.6 norm.3
  61.6 0.0 copy-start.2
  61.6 21.2 %all_to_all.37 = bf16[128,5,2,128]{3,2,1,0:T(2,128)(2,1)S(1)} all-to-all(bf16[128,5,2,128]{3,2,1,0:T(2,128)(2,1)S(1)} %bitcast.38), channel_id=1, replica_groups={{0,2,4,6,8,10,12,14,16,18,20,22,24,26,28,30,32,34,36,38,40,42,44,46,48,..., dimensions={0} | all-to-all | bytes 655360 | tf_op jit(solution)/shard_map/all_to_all | solution.py:208
  82.8 0.0 collective-permute-start.4
  82.8 1.0 right.3
  83.8 0.0 copy-done.2
  83.8 0.6 collective-permute-done.4
  84.4 1.7 %left.3 = (bf16[2304,128]{1,0:T(8,128)(2,1)}, s32[1]{0:T(128)}) custom-call(bf16[1280,128]{1,0:T(8,128)(2,1)S(1)} %bitcast.39, bf16[512,256]{1,0:T(8,128)(2,1)S(1)} %get-tuple-element.93.gp_ref, bf16[256,256]{1,0:T(8,128)(2,1)S(1)} %get-tuple-element.84.keep_ref, bf16[256,256]{1,0:T(8,128)(2,1)S(1)} %collective-permute-done.3.got_ref, ...), custom_call_target="tpu_custom_call" | custom-call | bytes 3000000 | tf_op jit(solution)/shard_map/left/pallas_call | solution.py:262
  86.1 6.8 %all-to-all-start.6 = ((bf16[128,9,2,128]{3,2,1,0:T(2,128)(2,1)}), bf16[128,9,2,128]{3,2,1,0:T(2,128)(2,1)S(1)}, u32[]{:S(2)}, u32[]{:S(2)}) async-start(bf16[128,9,2,128]{3,2,1,0:T(2,128)(2,1)} %bitcast.21), calls=%async_computation.6 | async-start | bytes 1179648 | tf_op jit(solution)/shard_map/all_to_all | solution.py:208
  93.6 20.6 %all-to-all-done.6 = bf16[128,9,2,128]{3,2,1,0:T(2,128)(2,1)S(1)} async-done(((bf16[128,9,2,128]{3,2,1,0:T(2,128)(2,1)}), bf16[128,9,2,128]{3,2,1,0:T(2,128)(2,1)S(1)}, u32[]{:S(2)}, u32[]{:S(2)}) %all-to-all-start.6) | async-done | bytes 589856 | tf_op jit(solution)/shard_map/all_to_all | solution.py:208
  114.2 1.0 unpack.3
  (3 shorter events, 0.1 us)
Async XLA Ops:
  37.1 2.1 %copy-start.4 = (bf16[128,128]{1,0:T(8,128)(2,1)S(1)}, bf16[128,128]{1,0:T(8,128)(2,1)}, u32[]{:S(2)}) copy-start(bf16[128,128]{1,0:T(8,128)(2,1)} %weight_ref.1) | copy-start | bytes 98308
  37.5 1.7 %copy-start = (bf16[32,32,128]{2,1,0:T(8,128)(2,1)S(1)}, bf16[32,32,128]{2,1,0:T(8,128)(2,1)}, u32[]{:S(2)}) copy-start(bf16[32,32,128]{2,1,0:T(8,128)(2,1)} %param.9) | copy-start | bytes 786436
  37.6 1.6 %copy-start.1 = (bf16[32,32,128]{2,1,0:T(8,128)(2,1)S(1)}, bf16[32,32,128]{2,1,0:T(8,128)(2,1)}, u32[]{:S(2)}) copy-start(bf16[32,32,128]{2,1,0:T(8,128)(2,1)} %param.11) | copy-start | bytes 786436
  37.6 1.6 %collective-permute-start.2 = (bf16[512,256]{1,0:T(8,128)(2,1)S(1)}, bf16[512,256]{1,0:T(8,128)(2,1)S(1)}, u32[]{:S(2)}, u32[]{:S(2)}) collective-permute-start(bf16[512,256]{1,0:T(8,128)(2,1)S(1)} %left_order.1.a_ref), channel_id=1, source_target_pairs={{0,1},{1,0},{2,3},{3,2},{4,5},{5,4},{6,7},{7,6},{8,9},{9,8},{10,11... | collective-permute-start | bytes 786440 | tf_op jit(solution)/shard_map/ppermute | solution.py:212
  38.4 1.6 %collective-permute-start.3 = (bf16[256,256]{1,0:T(8,128)(2,1)S(1)}, bf16[256,256]{1,0:T(8,128)(2,1)S(1)}, u32[]{:S(2)}, u32[]{:S(2)}) collective-permute-start(bf16[256,256]{1,0:T(8,128)(2,1)S(1)} %get-tuple-element.85.send_ref), channel_id=1, source_target_pairs={{0,1},{1,0},{2,3},{3,2},{4,5},{5,4},{6,7},{7,6},{8,9},{9,8},{10,11... | collective-permute-start | bytes 393224 | tf_op jit(solution)/shard_map/ppermute | solution.py:212
  61.6 22.2 %copy-start.2 = (bf16[1024,128]{1,0:T(8,128)(2,1)}, bf16[1024,128]{1,0:T(8,128)(2,1)S(1)}, u32[]{:S(2)}) copy-start(bf16[1024,128]{1,0:T(8,128)(2,1)S(1)} %get-tuple-element.92.gate_ref) | copy-start | bytes 786436
  82.8 1.6 %collective-permute-start.4 = (bf16[128,5,2,128]{3,2,1,0:T(2,128)(2,1)S(1)}, bf16[128,5,2,128]{3,2,1,0:T(2,128)(2,1)S(1)}, u32[]{:S(2)}, u32[]{:S(2)}) collective-permute-start(bf16[128,5,2,128]{3,2,1,0:T(2,128)(2,1)S(1)} %all_to_all.37), channel_id=1, source_target_pairs={{0,1},{1,0},{2,3},{3,2},{4,5},{5,4},{6,7},{7,6},{8,9},{9,8},{10,11... | collective-permute-start | bytes 983048 | tf_op jit(solution)/shard_map/ppermute | solution.py:212
  86.1 28.1 %all-to-all-start.6 = ((bf16[128,9,2,128]{3,2,1,0:T(2,128)(2,1)}), bf16[128,9,2,128]{3,2,1,0:T(2,128)(2,1)S(1)}, u32[]{:S(2)}, u32[]{:S(2)}) async-start(bf16[128,9,2,128]{3,2,1,0:T(2,128)(2,1)} %bitcast.21), calls=%async_computation.6 | async-start | bytes 1179648 | tf_op jit(solution)/shard_map/all_to_all | solution.py:208

commit v9 on v8

--- a/solution.py
+++ b/solution.py
@@ -147,9 +147,10 @@
     return jnp.sum(terms[0], axis=0, keepdims=True) + jnp.sum(terms[1], axis=0, keepdims=True)
 
 
-def right_kernel(core_ref, own_ref, a_ref, other_ref, gate_ref, gp_ref, sum_ref, out_ref, raw, flat):
+def right_kernel(core_ref, own_ref, a_ref, other_ref, gate_ref, keep_ref, gp_ref, sum_ref, out_ref, near_ref, raw, flat):
     core = core_ref[0]
     sum_ref[...] = jnp.broadcast_to(half_order(own_ref, raw, gp_ref), (8, 128))
+    near_ref[...] = jnp.dot(gp_ref[...], keep_ref[...], preferred_element_type=F32)
     turned = gp_ref[...].T
     for which, ref in enumerate((a_ref, other_ref)):
         parity = core if which == 0 else 1 - core
@@ -166,14 +167,13 @@
                     out_ref[where] = part.reshape(4, 8, 128).astype(BF16)
 
 
-def left_kernel(far_ref, gp_ref, keep_ref, got_ref, sum_ref, right_ref, out_ref, flag_ref, raw, gp, prod, out):
+def left_kernel(far_ref, near_ref, got_ref, sum_ref, right_ref, out_ref, flag_ref, raw, gp, prod, out):
     total = half_order(far_ref, raw, gp) + sum_ref[0:1, :]
     flag_ref[0] = (jnp.max(total) > 3e38).astype(jnp.int32)
     high, rest = split_halves(total)
     out[pl.ds(16, 128, stride=18), :] = jnp.broadcast_to(high, (128, 128))
     out[pl.ds(17, 128, stride=18), :] = jnp.broadcast_to(rest, (128, 128))
-    value = jnp.dot(gp_ref[...], keep_ref[...], preferred_element_type=F32)
-    value += jnp.dot(gp[...], got_ref[...], preferred_element_type=F32)
+    value = near_ref[...] + jnp.dot(gp[...], got_ref[...], preferred_element_type=F32)
     for g in range(2):
         prod[g] = value[:, g * 128 : (g + 1) * 128]
     for g in range(2):
@@ -252,20 +252,20 @@
         )(pair.reshape(flat), gates, ups, weight)
         own = exchange(grad_pair.reshape(128, 5, 2, 128))
         far = other_core(own)
-        half, total, right = call(
+        _, total, right, near = call(
             right_kernel,
-            [((512, 256), BF16), ((8, 128), F32), ((16, 8, 8, 128), BF16)],
-            [SM] + [VM] * 4,
+            [((512, 256), BF16), ((8, 128), F32), ((16, 8, 8, 128), BF16), ((512, 256), F32)],
+            [SM] + [VM] * 5,
             [((1280, 128), F32), ((4, 256, 128), F32)],
             "right",
-        )(core, own.reshape(1280, 128), a, other, grad_gate)
+        )(core, own.reshape(1280, 128), a, other, grad_gate, keep)
         grads, flag = call(
             left_kernel,
             [((2304, 128), BF16), ((1,), jnp.int32)],
-            [VM] * 6,
+            [VM] * 5,
             [((1280, 128), F32), ((512, 256), BF16), ((2, 512, 128), F32), ((2304, 128), F32)],
             "left",
-        )(far.reshape(1280, 128), half, keep, got, total, right)
+        )(far.reshape(1280, 128), near, got, total, right)
         grads = exchange(grads.reshape(128, 9, 2, 128))
         grad_left, grad_right, grad_weight = call(
             unpack_kernel,

time: 116 us -> 116 us (level)
  no operation moved by 1% of the time
where the time goes in v9:
time: 116 us
  blocking collectives  76.7 us (66%)
  waiting for transfers between devices  21.4 us (18%)
  starting transfers between devices  7.52 us (6%)
  Pallas kernels  7.38 us (6%)
  between operations  1.39 us (1%)
    all_to_all x3, blocking collectives, exchange(): lax.all_to_all(x, ('row', 'col'), 0, 0, axis_index_groups=SAME_CORE, tile...  76.7 us
    all_to_all x1, waiting for transfers between devices, exchange(): lax.all_to_all(x, ('row', 'col'), 0, 0, axis_index_groups=SAME_CORE, tile...  20.8 us
    all_to_all x1, starting transfers between devices, exchange(): lax.all_to_all(x, ('row', 'col'), 0, 0, axis_index_groups=SAME_CORE, tile...  6.85 us
  transfers between devices with their start and end apart: 4, of which 4 were waited for; matrix products, arithmetic and copies ran while one was open for 0% of the time, Pallas kernels for 2%

profile of v9, /device:TPU:6, one launch (start us, length us, event | category | flops | bytes accessed | tf_op | source)
XLA Modules:
  0.0 115.6 jit_solution(3345501602324735764)
XLA Ops:
  0.6 1.1 pad_maximum_fusion.in_ref
  1.7 0.7 pack.1
  2.4 34.7 %all_to_all.35 = bf16[128,16,128]{2,1,0:T(8,128)(2,1)S(1)} all-to-all(bf16[128,16,128]{2,1,0:T(8,128)(2,1)S(1)} %pack.1), channel_id=1, replica_groups={{0,2,4,6,8,10,12,14,16,18,20,22,24,26,28,30,32,34,36,38,40,42,44,46,48,..., dimensions={0} | all-to-all | bytes 1048576 | tf_op jit(solution)/shard_map/all_to_all | solution.py:208
  37.1 0.0 copy-start.4
  37.1 0.4 left_order.1.a_ref
  37.5 0.0 copy-start
  37.6 0.0 copy-start.1
  37.6 0.1 collective-permute-start.2
  37.7 0.7 right_order.1
  38.4 0.6 collective-permute-start.3
  39.0 0.2 collective-permute-done.2.other_ref
  39.2 0.0 copy-done.4
  39.2 0.0 copy-done
  39.2 0.0 copy-done.1
  39.2 0.6 pair.3
  39.8 0.2 collective-permute-done.3.got_ref
  40.0 20.9 %all_to_all.36 = f16[128,8,128]{2,1,0:T(8,128)(2,1)S(1)} all-to-all(f16[128,8,128]{2,1,0:T(8,128)(2,1)S(1)} %bitcast.41), channel_id=1, replica_groups={{0,2,4,6,8,10,12,14,16,18,20,22,24,26,28,30,32,34,36,38,40,42,44,46,48,..., dimensions={0} | all-to-all | bytes 524288 | tf_op jit(solution)/shard_map/all_to_all | solution.py:208
  60.9 0.6 norm.3
  61.6 0.0 copy-start.2
  61.6 21.2 %all_to_all.37 = bf16[128,5,2,128]{3,2,1,0:T(2,128)(2,1)S(1)} all-to-all(bf16[128,5,2,128]{3,2,1,0:T(2,128)(2,1)S(1)} %bitcast.38), channel_id=1, replica_groups={{0,2,4,6,8,10,12,14,16,18,20,22,24,26,28,30,32,34,36,38,40,42,44,46,48,..., dimensions={0} | all-to-all | bytes 655360 | tf_op jit(solution)/shard_map/all_to_all | solution.py:208
  82.7 0.0 collective-permute-start.4
  82.7 1.5 %right.3 = (bf16[512,256]{1,0:T(8,128)(2,1)}, f32[8,128]{1,0:T(8,128)S(1)}, bf16[16,8,8,128]{3,2,1,0:T(8,128)(2,1)S(1)}, f32[512,256]{1,0:T(8,128)S(1)}) custom-call(s32[1]{0:T(128)} %bitcast.9.core_ref, bf16[1280,128]{1,0:T(8,128)(2,1)S(1)} %bitcast.33, bf16[512,256]{1,0:T(8,128)(2,1)S(1)} %left_order.1.a_ref, ...), custom_call_target="tpu_custom_call" | custom-call | bytes 3000000 | tf_op jit(solution)/shard_map/right/pallas_call | solution.py:255
  84.3 0.0 copy-done.2
  84.3 0.1 collective-permute-done.4
  84.4 1.8 %left.3 = (bf16[2304,128]{1,0:T(8,128)(2,1)}, s32[1]{0:T(128)}) custom-call(bf16[1280,128]{1,0:T(8,128)(2,1)S(1)} %bitcast.39, f32[512,256]{1,0:T(8,128)S(1)} %get-tuple-element.93.near_ref, bf16[256,256]{1,0:T(8,128)(2,1)S(1)} %collective-permute-done.3.got_ref, f32[8,128]{1,0:T(8,128)S(1)} %get-tuple-element.95.sum_ref, ...), custom_call_target="tpu_custom_call" | custom-call | bytes 3000000 | tf_op jit(solution)/shard_map/left/pallas_call | solution.py:262
  86.2 6.8 %all-to-all-start.6 = ((bf16[128,9,2,128]{3,2,1,0:T(2,128)(2,1)}), bf16[128,9,2,128]{3,2,1,0:T(2,128)(2,1)S(1)}, u32[]{:S(2)}, u32[]{:S(2)}) async-start(bf16[128,9,2,128]{3,2,1,0:T(2,128)(2,1)} %bitcast.21), calls=%async_computation.6 | async-start | bytes 1179648 | tf_op jit(solution)/shard_map/all_to_all | solution.py:208
  93.7 20.8 %all-to-all-done.6 = bf16[128,9,2,128]{3,2,1,0:T(2,128)(2,1)S(1)} async-done(((bf16[128,9,2,128]{3,2,1,0:T(2,128)(2,1)}), bf16[128,9,2,128]{3,2,1,0:T(2,128)(2,1)S(1)}, u32[]{:S(2)}, u32[]{:S(2)}) %all-to-all-start.6) | async-done | bytes 589856 | tf_op jit(solution)/shard_map/all_to_all | solution.py:208
  114.5 1.0 unpack.3
  (3 shorter events, 0.1 us)
Async XLA Ops:
  37.1 2.1 %copy-start.4 = (bf16[128,128]{1,0:T(8,128)(2,1)S(1)}, bf16[128,128]{1,0:T(8,128)(2,1)}, u32[]{:S(2)}) copy-start(bf16[128,128]{1,0:T(8,128)(2,1)} %weight_ref.1) | copy-start | bytes 98308
  37.5 1.7 %copy-start = (bf16[32,32,128]{2,1,0:T(8,128)(2,1)S(1)}, bf16[32,32,128]{2,1,0:T(8,128)(2,1)}, u32[]{:S(2)}) copy-start(bf16[32,32,128]{2,1,0:T(8,128)(2,1)} %param.9) | copy-start | bytes 786436
  37.6 1.6 %copy-start.1 = (bf16[32,32,128]{2,1,0:T(8,128)(2,1)S(1)}, bf16[32,32,128]{2,1,0:T(8,128)(2,1)}, u32[]{:S(2)}) copy-start(bf16[32,32,128]{2,1,0:T(8,128)(2,1)} %param.11) | copy-start | bytes 786436
  37.6 1.6 %collective-permute-start.2 = (bf16[512,256]{1,0:T(8,128)(2,1)S(1)}, bf16[512,256]{1,0:T(8,128)(2,1)S(1)}, u32[]{:S(2)}, u32[]{:S(2)}) collective-permute-start(bf16[512,256]{1,0:T(8,128)(2,1)S(1)} %left_order.1.a_ref), channel_id=1, source_target_pairs={{0,1},{1,0},{2,3},{3,2},{4,5},{5,4},{6,7},{7,6},{8,9},{9,8},{10,11... | collective-permute-start | bytes 786440 | tf_op jit(solution)/shard_map/ppermute | solution.py:212
  38.4 1.6 %collective-permute-start.3 = (bf16[256,256]{1,0:T(8,128)(2,1)S(1)}, bf16[256,256]{1,0:T(8,128)(2,1)S(1)}, u32[]{:S(2)}, u32[]{:S(2)}) collective-permute-start(bf16[256,256]{1,0:T(8,128)(2,1)S(1)} %get-tuple-element.85.send_ref), channel_id=1, source_target_pairs={{0,1},{1,0},{2,3},{3,2},{4,5},{5,4},{6,7},{7,6},{8,9},{9,8},{10,11... | collective-permute-start | bytes 393224 | tf_op jit(solution)/shard_map/ppermute | solution.py:212
  61.6 22.7 %copy-start.2 = (bf16[1024,128]{1,0:T(8,128)(2,1)}, bf16[1024,128]{1,0:T(8,128)(2,1)S(1)}, u32[]{:S(2)}) copy-start(bf16[1024,128]{1,0:T(8,128)(2,1)S(1)} %get-tuple-element.92.gate_ref) | copy-start | bytes 786436
  82.7 1.6 %collective-permute-start.4 = (bf16[128,5,2,128]{3,2,1,0:T(2,128)(2,1)S(1)}, bf16[128,5,2,128]{3,2,1,0:T(2,128)(2,1)S(1)}, u32[]{:S(2)}, u32[]{:S(2)}) collective-permute-start(bf16[128,5,2,128]{3,2,1,0:T(2,128)(2,1)S(1)} %all_to_all.37), channel_id=1, source_target_pairs={{0,1},{1,0},{2,3},{3,2},{4,5},{5,4},{6,7},{7,6},{8,9},{9,8},{10,11... | collective-permute-start | bytes 983048 | tf_op jit(solution)/shard_map/ppermute | solution.py:212
  86.2 28.3 %all-to-all-start.6 = ((bf16[128,9,2,128]{3,2,1,0:T(2,128)(2,1)}), bf16[128,9,2,128]{3,2,1,0:T(2,128)(2,1)S(1)}, u32[]{:S(2)}, u32[]{:S(2)}) async-start(bf16[128,9,2,128]{3,2,1,0:T(2,128)(2,1)} %bitcast.21), calls=%async_computation.6 | async-start | bytes 1179648 | tf_op jit(solution)/shard_map/all_to_all | solution.py:208
